TPU v7x, 128 devices: a whole 4x4x4 slice. The times are simulated.
128 devices in a mesh: grp: 8 (over y, core), blk: 16 (over x, z).
Axes of the slice: x: 4, y: 4, z: 4, core: 2. Of those that a mesh axis runs over, the one named last changes fastest.
Arguments:
- embeddings: float32 [65536, 1024], P(('grp', 'blk'))
- cluster_id: int32 [65536], P(('grp', 'blk')), may hold values from 0 to 63, as said below
- cluster_group: int32 [64], replicated, may hold values from 0 to 7, as said below
Outputs:
- max_cos: float32 [65536], P(('grp', 'blk'))
- log_mass: float32 [65536], P(('grp', 'blk'))
Inputs may be any that keep to these rules, and one draw needn't show every extreme that they name: `cluster_id`: among the rows of one device, at most 96 name clusters that cluster_group maps to one group; for some group exactly 96. `cluster_group`: each group owns 8 clusters.
All inputs are finite; a program needn't handle non-finite values.
Results may differ from a plain program's by a relative error of at most 0.00042.
Values may be sent and summed in bfloat16 or wider, within the bound.
A program may use at most 128 MiB of HBM per device.

v0:
```python
import jax
import jax.numpy as jnp
from jax import lax
from jax.sharding import PartitionSpec as P


def pair_scores(left, right):
    return lax.dot_general(
        left, right, (((1,), (1,)), ((), ())), preferred_element_type=jnp.float32
    )


def body(embeddings, cluster_id, cluster_group):
    rows, width = embeddings.shape
    groups = lax.axis_size("grp")
    capacity = rows * 3 // (2 * groups)
    unit = (
        embeddings * lax.rsqrt(jnp.sum(embeddings * embeddings, axis=1, keepdims=True) + 1e-06)
    ).astype(jnp.bfloat16)
    clusters = cluster_group.shape[0]
    member = cluster_id[:, None] == lax.broadcasted_iota(jnp.int32, (rows, clusters), 1)
    target = jnp.sum(jnp.where(member, cluster_group[None, :], 0), axis=1)
    picks = (target[:, None] == lax.broadcasted_iota(jnp.int32, (rows, groups), 1)).astype(
        jnp.int32
    )
    before = jnp.cumsum(picks, axis=0) - picks
    position = jnp.sum(before * picks, axis=1)
    slot = target * capacity + position
    outgoing = jnp.zeros((groups * capacity, width), jnp.bfloat16).at[slot].set(unit)
    labels = jnp.full((groups * capacity,), -1, jnp.int32).at[slot].set(cluster_id)
    incoming, owners = (
        lax.all_to_all(
            outgoing.reshape(groups, capacity, width),
            "grp",
            split_axis=0,
            concat_axis=0,
            tiled=True,
        ),
        lax.all_to_all(
            labels.reshape(groups, capacity), "grp", split_axis=0, concat_axis=0, tiled=True
        ),
    )
    local = incoming.reshape(groups * capacity, width)
    tags = owners.reshape(groups * capacity)
    count = local.shape[0]
    valid = tags >= 0
    sharpness = 20.0
    floor_value = jnp.full((count,), -1.0, jnp.float32)
    nothing = jnp.zeros((count,), jnp.float32)
    base = lax.axis_index("blk") * count
    units_p = lax.all_gather(local, "blk", axis=0, tiled=True)
    tags_p = lax.all_gather(tags, "blk", axis=0, tiled=True)
    width_p = units_p.shape[0]
    scores = pair_scores(local, units_p)
    same = (tags[:, None] == tags_p[None, :]) & valid[:, None]
    selfs = base + lax.broadcasted_iota(jnp.int32, (count, width_p), 0) == lax.broadcasted_iota(
        jnp.int32, (count, width_p), 1
    )
    other = same & jnp.logical_not(selfs)
    best = jnp.max(jnp.where(other, scores, -1.0), axis=1)
    total = jnp.sum(jnp.where(other, jnp.exp(sharpness * scores), 0.0), axis=1)
    best, total = (jnp.maximum((floor_value, nothing)[0], best), total)
    mass = jnp.log(1.0 + total)
    back_max, back_mass = (
        lax.all_to_all(
            best.reshape(groups, capacity), "grp", split_axis=0, concat_axis=0, tiled=True
        ),
        lax.all_to_all(
            mass.reshape(groups, capacity), "grp", split_axis=0, concat_axis=0, tiled=True
        ),
    )
    max_cos = back_max.reshape(-1)[slot]
    log_mass = back_mass.reshape(-1)[slot]
    return (max_cos, log_mass)


def solution(mesh):
    in_specs = (P(("grp", "blk"), None), P(("grp", "blk")), P())
    out_specs = (P(("grp", "blk")), P(("grp", "blk")))
    return jax.shard_map(body, mesh=mesh, in_specs=in_specs, out_specs=out_specs, check_vma=False)
```

profile of v0, /device:TPU:1, one launch (start us, length us, event | category | flops | bytes accessed | tf_op | source)
XLA Modules:
  0.0 266.0 jit_solution(12415118805373940523)
XLA Ops:
  7.2 0.8 select_reduce_fusion.2
  8.0 1.1 reduce-window.6
  9.5 1.8 multiply_reduce_fusion
  11.3 4.1 %scatter_custom_fusion.1 = bf16[768,1024]{1,0:T(8,128)(2,1)S(1)} fusion(s32[512]{0:T(512)S(1)} %bitcast.23, f32[512,1024]{1,0:T(8,128)} %param.3, f32[512]{0:T(512)S(1)} %add_rsqrt_fusion, bf16[]{:T(256)} %constant.17.clone.1), kind=kCustom, calls=%fused_computation.11 | custom fusion | flops 1048576 | bytes 3672066 | tf_op jit(solution)/shard_map/scatter | solution.py:29
  15.5 26.6 %all_to_all.26 = bf16[8,96,1024]{2,1,0:T(8,128)(2,1)} all-to-all(bf16[8,96,1024]{2,1,0:T(8,128)(2,1)S(1)} %bitcast.19), channel_id=1, replica_groups=mesh['grp'=8,'blk'=16] {'grp'}, dimensions={0} | all-to-all | bytes 3145728 | tf_op jit(solution)/shard_map/all_to_all | solution.py:32
  42.1 2.6 scatter_custom_fusion
  44.8 0.7 all_to_all.17
  45.4 4.2 %all-to-all-start = ((s32[8,1,96]{2,1,0:T(1,128)}), s32[8,1,96]{2,1,0:T(1,128)S(1)}, u32[]{:S(2)}, u32[]{:S(2)}) async-start(s32[8,1,96]{2,1,0:T(1,128)} %all_to_all.17), calls=%async_computation | async-start | bytes 8192 | tf_op jit(solution)/shard_map/all_to_all | solution.py:39
  49.6 4.6 %all-to-all-done = s32[8,1,96]{2,1,0:T(1,128)S(1)} async-done(((s32[8,1,96]{2,1,0:T(1,128)}), s32[8,1,96]{2,1,0:T(1,128)S(1)}, u32[]{:S(2)}, u32[]{:S(2)}) %all-to-all-start) | async-done | bytes 3104 | tf_op jit(solution)/shard_map/all_to_all | solution.py:39
  54.7 0.7 reduce.13
  55.6 22.0 %all-gather = s32[16,1,768]{2,1,0:T(1,128)S(1)} all-gather(s32[1,1,768]{2,1,0:T(1,128)S(1)} %reshape.154), channel_id=1, replica_groups=mesh['grp'=8,'blk'=16] {'blk'}, dimensions={0}, use_global_device_ids=true | all-gather | bytes 52224 | tf_op jit(solution)/shard_map/all_gather | solution.py:52
  77.5 120.1 %all-gather.3.cloned.1.call-done = bf16[12288,1024]{1,0:T(8,128)(2,1)} async-done(((bf16[768,1024]{1,0:T(8,128)(2,1)}), bf16[12288,1024]{1,0:T(8,128)(2,1)}) %all-gather.3.cloned.1.call-update) | async-done | bytes 25165840 | tf_op jit(solution)/shard_map/all_gather | solution.py:51
  197.6 35.2 %select_reduce_fusion = (f32[768]{0:T(1024)S(1)}, f32[768]{0:T(1024)S(1)}) fusion(s32[768]{0:T(1024)S(1)} %iota_add_fusion, pred[768]{0:T(1024)(128)(4,1)S(1)} %broadcast_compare_fusion, s32[12288]{0:T(1024)S(1)} %bitcast.20, s32[768]{0:T(1024)S(1)} %eq.49, bf16[768,1024]{1,0:T(8,128)(2,1)} %bitcast.18, bf16[12288,1024]{1,0:T(8,128)(2,1)} %all-gather.3.cloned.1.call-done), kind=kOutput, calls=%fused_computation.4 | convolution fusion | flops 19421724672 | bytes 26800896 | tf_op jit(solution)/shard_map/dot_general | solution.py:8
  232.8 0.7 log.15
  233.5 5.0 %all-to-all-start.3 = ((f32[8,1,96]{2,1,0:T(1,128)}), f32[8,1,96]{2,1,0:T(1,128)S(1)}, u32[]{:S(2)}, u32[]{:S(2)}) async-start(f32[8,1,96]{2,1,0:T(1,128)} %log.15), calls=%async_computation.3 | async-start | bytes 8192 | tf_op jit(solution)/shard_map/all_to_all | solution.py:68
  238.5 0.7 max_broadcast_in_dim.15
  239.1 3.9 %all-to-all-done.3 = f32[8,1,96]{2,1,0:T(1,128)S(1)} async-done(((f32[8,1,96]{2,1,0:T(1,128)}), f32[8,1,96]{2,1,0:T(1,128)S(1)}, u32[]{:S(2)}, u32[]{:S(2)}) %all-to-all-start.3) | async-done | bytes 3104 | tf_op jit(solution)/shard_map/all_to_all | solution.py:68
  243.0 3.9 %all-to-all-start.2 = ((f32[8,1,96]{2,1,0:T(1,128)}), f32[8,1,96]{2,1,0:T(1,128)S(1)}, u32[]{:S(2)}, u32[]{:S(2)}) async-start(f32[8,1,96]{2,1,0:T(1,128)} %max_broadcast_in_dim.15), calls=%async_computation.2 | async-start | bytes 8192 | tf_op jit(solution)/shard_map/all_to_all | solution.py:65
  247.0 0.5 broadcast.101
  247.5 0.7 reduce.15
  248.2 3.3 %all-to-all-done.2 = f32[8,1,96]{2,1,0:T(1,128)S(1)} async-done(((f32[8,1,96]{2,1,0:T(1,128)}), f32[8,1,96]{2,1,0:T(1,128)S(1)}, u32[]{:S(2)}, u32[]{:S(2)}) %all-to-all-start.2) | async-done | bytes 3104 | tf_op jit(solution)/shard_map/all_to_all | solution.py:65
  251.6 0.7 reduce.14
  252.3 3.4 %gather_fusion.1 = f32[512]{0:T(512)} fusion(f32[768]{0:T(1024)S(1)} %reshape.121, s32[1024]{0:T(1024)S(1)} %pad_clamp_fusion), kind=kCustom, calls=%fused_computation.1 | custom fusion | bytes 6144 | tf_op jit(solution)/shard_map/gather | solution.py:73
  255.7 3.4 %gather_fusion = f32[512]{0:T(512)} fusion(f32[768]{0:T(1024)S(1)} %reshape.120, s32[1024]{0:T(1024)S(1)} %pad_clamp_fusion), kind=kCustom, calls=%fused_computation | custom fusion | bytes 6144 | tf_op jit(solution)/shard_map/gather | solution.py:72
  (20 shorter events, 1.3 us)
Async XLA Ops:
  7.2 190.4 %all-gather.3.cloned.1.call-start = ((), (), s32[]{:S(2)}) async-start(), calls=%async_computation.4 | async-start | bytes 26738688 | tf_op jit(solution)/shard_map/all_gather | solution.py:51
  45.4 8.8 %all-to-all-start = ((s32[8,1,96]{2,1,0:T(1,128)}), s32[8,1,96]{2,1,0:T(1,128)S(1)}, u32[]{:S(2)}, u32[]{:S(2)}) async-start(s32[8,1,96]{2,1,0:T(1,128)} %all_to_all.17), calls=%async_computation | async-start | bytes 8192 | tf_op jit(solution)/shard_map/all_to_all | solution.py:39
  233.5 9.5 %all-to-all-start.3 = ((f32[8,1,96]{2,1,0:T(1,128)}), f32[8,1,96]{2,1,0:T(1,128)S(1)}, u32[]{:S(2)}, u32[]{:S(2)}) async-start(f32[8,1,96]{2,1,0:T(1,128)} %log.15), calls=%async_computation.3 | async-start | bytes 8192 | tf_op jit(solution)/shard_map/all_to_all | solution.py:68
  243.0 8.5 %all-to-all-start.2 = ((f32[8,1,96]{2,1,0:T(1,128)}), f32[8,1,96]{2,1,0:T(1,128)S(1)}, u32[]{:S(2)}, u32[]{:S(2)}) async-start(f32[8,1,96]{2,1,0:T(1,128)} %max_broadcast_in_dim.15), calls=%async_computation.2 | async-start | bytes 8192 | tf_op jit(solution)/shard_map/all_to_all | solution.py:65
Sparse Core Ops, SparseCore 0:
  42.3 155.2 all-gather.2
where the time goes:
time: 266 us
  waiting for transfers between devices  132 us (50%)
  blocking collectives  48.6 us (18%)
  matrix products  35.2 us (13%)
  between operations  14.1 us (5%)
  starting transfers between devices  13.1 us (5%)
  local copies, waits for them, and re-layouts  13 us (5%)
  other arithmetic  10 us (4%)
    all_gather x1, waiting for transfers between devices, body(): units_p = lax.all_gather(local, 'blk', axis=0, tiled=True)  120 us
    dot_general x1, matrix products, pair_scores(): lax.dot_general(left, right, (((1,), (1,)), ((), ())), preferred_element_...  35.2 us
    all_to_all x1, blocking collectives, body(): lax.all_to_all(outgoing.reshape(groups, capacity, width), 'grp', split_ax...  26.6 us
    all_gather x1, blocking collectives, body(): tags_p = lax.all_gather(tags, 'blk', axis=0, tiled=True)  22 us
  transfers between devices with their start and end apart: 4, of which 4 were waited for; matrix products, arithmetic and copies ran while one was open for 2% of the time, Pallas kernels for 0%

commit v1 on v0

v1 whole, which is shorter than its diff:
```python
import functools

import jax
import jax.numpy as jnp
from jax import lax
from jax.experimental import pallas as pl
from jax.experimental.pallas import tpu as pltpu
from jax.sharding import PartitionSpec as P

MESH = pl.DeviceIdType.MESH
F32 = jnp.float32
BF16 = jnp.bfloat16
GROUPS = 8
SLOTS = 6
MASKED = -30.0
ORDER = (0, 1, 3, 2)

ZB, XB, CB = "z", "x", "c"


def program():
    steps = []

    def ev(*names):
        steps.extend(("ev", kind, q) for kind, qs in names for q in qs)

    def full(i, a, j, b):
        steps.append(("tile", i, a, j, b))

    def self_tile(a):
        steps.append(("self", a))

    ev(("E0", [0, 1]), ("E1", [0, 1]), ("E0", [2, 3]))
    self_tile(0)
    ev(("E1", [2]), ("E2", [0]), ("E0", [4, 5]), ("E2", [1]), ("E1", [3]))
    full(0, 0, 1, 0)
    ev(("E4", [0, 1, 2, 3]), ("E2", [2]), ("E1", [4]))
    ev(("E2", [3]), ("E1", [5]), ("E3", [0, 1, 2, 3]))
    full(3, 0, 1, 0)
    ev(("E2", [4]), ("E5", [0, 1, 2, 3]))
    full(3, 0, 4, 0)
    ev(("E2", [5]), ("E0", [6]))
    full(3, 0, 5, 0)
    ev(("E0", [7]), ("E1", [6]))
    self_tile(1)
    full(0, 0, 0, 1)
    ev(("E1", [7]), ("E2", [6]))
    full(0, 1, 1, 0)
    full(0, 1, 2, 0)
    ev(("E2", [7]))
    full(0, 1, 3, 0)
    full(0, 1, 5, 0)
    full(0, 1, 4, 0)
    ev(("E4", [4, 5, 6, 7]))
    full(0, 0, 1, 1)
    full(0, 1, 1, 1)
    full(3, 0, 1, 1)
    full(3, 0, 4, 1)
    full(0, CB, 4, CB)
    full(5, 0, 1, 1)
    ev(("E5", [4, 5, 6, 7]))
    full(0, ZB, 2, ZB)
    full(3, 0, 2, 1)
    full(3, 0, 5, 1)
    full(0, CB, 5, CB)
    full(5, 0, 2, 1)
    full(5, CB, 2, CB)
    full(5, CB, 1, CB)
    ev(("E3", [4, 5, 6, 7]))
    full(3, 1, 1, 0)
    full(3, 1, 1, 1)
    full(0, XB, 3, XB)
    full(3, XB, 2, XB)
    full(3, 1, 5, 0)
    full(3, 1, 5, 1)
    full(3, 1, 4, 0)
    full(3, 1, 4, 1)
    return steps


ROWSLOT = {0: 0, 3: 1, 5: 2}


def kernel(
    cap, cid_ref, cg_ref, emb_ref, best_ref, mass_ref,
    emb, unit, hot, outgo, sh, tagout, tagin, ct, rowtag,
    rowmax, rowsum, colmax, colsum, msg, rmsg, res, back, ids,
    in_sem, a_s, a_r, f_s, f_r, t_s, t_r, ct_s, ct_r, m_s, m_r, b_s, b_r,
):
    rows, width = emb.shape
    half = 4 * cap
    lanes = 128
    g, b = lax.axis_index("grp"), lax.axis_index("blk")
    y, c = g // 2, g % 2
    x, z = b // 4, b % 4
    h, xb = x // 2, x % 2
    xn = 2 * h + 1 - xb
    step = 2 * c - 1
    zf = (z + step + 4) % 4
    zb = (z - step + 4) % 4
    z2 = (z + 2) % 4
    x3 = 3 - x

    def dev(px, py, pz, pc):
        return {"grp": 2 * py + pc, "blk": 4 * px + pz}

    z3 = z + 2 * c - 4 * ((z + 2 * c) // 4)
    holder = {
        1: dev(x, y, zf, c), 2: dev(x, y, z2, c), 3: dev(xn, y, z3, c),
        4: dev(x, y, z, 1 - c), 5: dev(x, y, zf, 1 - c),
    }
    owner = dict(holder)
    owner[1] = dev(x, y, zb, c)

    barrier = pltpu.get_barrier_semaphore()
    friends = []
    for dy in range(4):
        yd = (y + dy) % 4
        for pc in (0, 1):
            if dy:
                friends.append(dev(x, yd, z, pc))
            friends.append(dev(x3, yd, z, pc))
    friends += [
        dev(x, y, z, 1 - c), dev(x, y, zf, c), dev(x, y, zb, c), dev(x, y, z2, c),
        dev(xn, y, z, c), dev(xn, y, z2, c), dev(x, y, zf, 1 - c),
    ]
    for d in friends:
        pl.semaphore_signal(barrier, inc=1, device_id=d, device_id_type=MESH)

    parts = 4
    size = rows // parts

    def load(k):
        return pltpu.make_async_copy(
            emb_ref.at[pl.ds(k * size, size)], emb.at[pl.ds(k * size, size)], in_sem.at[k]
        )

    for k in range(parts):
        load(k).start()

    plan = program()
    tiles = [s for s in plan if s[0] != "ev"]
    bits = {ZB: z // 2, XB: xb, CB: c}

    def pick(t, values):
        value = 0
        for k, (base, bit) in enumerate(values):
            value = jnp.where(t == k, base + (bits[bit] if bit in bits else bit), value)
        return value

    def operands(t):
        work = [s[1:] if s[0] == "tile" else (0, 0, 0, 0) for s in tiles]
        ri = pick(t, [(2 * ROWSLOT[i], a) for i, a, _, _ in work])
        i = ri + jnp.where(ri < 2, 0, jnp.where(ri < 4, 4, 6))
        j = pick(t, [(2 * j, a) for _, _, j, a in work])
        return ri, i, j

    cid = cid_ref[...]
    group = jnp.zeros(cid.shape, jnp.int32)
    for k in range(cg_ref.shape[0]):
        group = jnp.where(cid == k, cg_ref[k], group)
    dy = ((group >> 1) - y) & 3
    order = jnp.where(dy == 0, 0, jnp.where(dy == 1, 1, jnp.where(dy == 3, 2, 3)))
    other = jnp.where((group & 1) == h, 0, 1)
    target = 2 * order + other
    picks = jnp.where(
        lax.broadcasted_iota(jnp.int32, (GROUPS, rows), 0) == target, 1.0, 0.0
    ).astype(F32)
    earlier = jnp.where(
        lax.broadcasted_iota(jnp.int32, (rows, rows), 0)
        < lax.broadcasted_iota(jnp.int32, (rows, rows), 1),
        1.0,
        0.0,
    ).astype(BF16)
    before = jnp.dot(picks.astype(BF16), earlier, preferred_element_type=F32)
    rank = jnp.sum(picks * before, axis=0, keepdims=True).astype(jnp.int32)
    place = target * cap + rank
    hot[...] = jnp.where(
        lax.broadcasted_iota(jnp.int32, (GROUPS * cap, rows), 0) == place, 1.0, 0.0
    ).astype(BF16)
    ids[...] = jnp.zeros(ids.shape, jnp.int32)
    for k in range(rows // lanes):
        ids[0, k : k + 1, :] = target[:, k * lanes : (k + 1) * lanes]
        ids[1, k : k + 1, :] = rank[:, k * lanes : (k + 1) * lanes]

    names = jnp.broadcast_to((cid + 1).astype(F32), (8, rows)).astype(BF16)
    tags = lax.dot_general(
        names, hot[...], (((1,), (1,)), ((), ())), preferred_element_type=F32
    )
    tagout[...] = jnp.zeros(tagout.shape, F32)
    for k in range(GROUPS):
        tagout[k, :, 0:cap] = tags[:, k * cap : (k + 1) * cap]

    rowmax[...] = jnp.full(rowmax.shape, -1.0, F32)
    colmax[...] = jnp.full(colmax.shape, -1.0, F32)
    rowsum[...] = jnp.zeros(rowsum.shape, F32)
    colsum[...] = jnp.zeros(colsum.shape, F32)
    res[...] = jnp.zeros(res.shape, F32)
    msg[...] = jnp.zeros(msg.shape, F32)

    pl.semaphore_wait(barrier, len(friends))

    def chunk(slot, q):
        return sh.at[2 * slot + q // 4, pl.ds((q % 4) * cap, cap)]

    def dest(n):
        yd = (y + ORDER[n // 2]) % 4
        return dev(x, yd, z, 0) if n % 2 == 0 else dev(x3, yd, z, 1)

    def landing(n):
        q = 2 * (n // 2) + c
        return sh.at[(n // 2) // 2, pl.ds((2 * ((n // 2) % 2) + c) * cap, cap)], q

    def send_tag(n):
        q = 2 * (n // 2) + c
        return pltpu.make_async_remote_copy(
            tagout.at[n], tagin.at[q], t_s.at[n], t_r.at[q], device_id=dest(n), device_id_type=MESH
        )

    def send_rows(n):
        dst, q = landing(n)
        return pltpu.make_async_remote_copy(
            outgo.at[pl.ds(n * cap, cap)], dst, a_s.at[n], a_r.at[q],
            device_id=dest(n), device_id_type=MESH,
        )

    keep_tag = pltpu.make_async_copy(tagout.at[0], tagin.at[0], t_r.at[0])
    keep_rows = pltpu.make_async_copy(outgo.at[pl.ds(0, cap)], chunk(0, 0), a_r.at[0])

    def start(n, remote, local):
        if n:
            remote.start()
        else:
            pl.when(c == 0)(local.start)
            pl.when(c == 1)(remote.start)

    for n in range(GROUPS):
        start(n, send_tag(n), keep_tag)

    for k in range(parts):
        load(k).wait()
        v = emb[pl.ds(k * size, size)]
        scale = lax.rsqrt(jnp.sum(v * v, axis=1, keepdims=True) + 1e-06)
        unit[pl.ds(k * size, size)] = (v * scale).astype(BF16)
    for k in range(GROUPS // 2):
        outgo[pl.ds(2 * k * cap, 2 * cap)] = jnp.dot(
            hot[pl.ds(2 * k * cap, 2 * cap)], unit[...], preferred_element_type=F32
        ).astype(BF16)
        for n in (2 * k, 2 * k + 1):
            start(n, send_rows(n), keep_rows)

    def landed(ref, sem):
        pltpu.make_async_copy(ref, ref, sem).wait()

    for q in range(GROUPS):
        landed(tagin.at[q], t_r.at[q])
        ct[q // 4, :, (q % 4) * cap : (q % 4 + 1) * cap] = tagin[q, :, 0:cap]

    def send_ct(j):
        return pltpu.make_async_remote_copy(
            ct.at[pl.ds(0, 2)], ct.at[pl.ds(2 * j, 2)], ct_s.at[j - 1], ct_r.at[j - 1],
            device_id=holder[j], device_id_type=MESH,
        )

    for j in range(1, SLOTS):
        send_ct(j).start()

    def row_tags(slot):
        for a in (0, 1):
            for k in range(half // lanes):
                v = ct[2 * slot + a, 0:1, k * lanes : (k + 1) * lanes]
                v = jnp.where(v == 0.0, -1.0, v)
                rowtag[2 * ROWSLOT[slot] + a, pl.ds(k * lanes, lanes), :] = jnp.transpose(
                    jnp.broadcast_to(v, (lanes, lanes))
                )

    row_tags(0)
    for j in range(1, SLOTS):
        landed(ct.at[pl.ds(2 * j, 2)], ct_r.at[j - 1])
    row_tags(3)
    row_tags(5)

    def forward(src, slot, q, to):
        return pltpu.make_async_remote_copy(
            chunk(src, q), chunk(slot, q), f_s.at[slot - 1, q], f_r.at[slot - 1, q],
            device_id=to, device_id_type=MESH,
        )

    ahead, across, sibling = dev(x, y, zf, c), dev(xn, y, z, c), dev(x, y, z, 1 - c)

    def event(kind, q):
        slot = int(kind[1])
        sem = a_r.at[q] if slot == 0 else f_r.at[slot - 1, q]
        landed(chunk(slot, q), sem)
        if slot == 0:
            forward(0, 1, q, ahead).start()
            pl.when(c == 0)(forward(0, 3, q, across).start)
            forward(0, 4, q, sibling).start()
        if slot == 1:
            forward(1, 2, q, ahead).start()
            forward(1, 5, q, sibling).start()
        if slot == 2:
            pl.when(c == 1)(forward(2, 3, q, across).start)

    def cut(ref, k):
        return ref[:, k * lanes : (k + 1) * lanes]

    blocks = half // lanes

    def scores(i, j):
        return lax.dot_general(
            sh[i], sh[j], (((1,), (1,)), ((), ())), preferred_element_type=F32
        )

    def tile(ri, i, j):
        s = scores(i, j)
        cm = [colmax[j, :, k * lanes : (k + 1) * lanes] for k in range(blocks)]
        cs = [colsum[j, :, k * lanes : (k + 1) * lanes] for k in range(blocks)]
        tag = [ct[j, 0:1, k * lanes : (k + 1) * lanes] for k in range(blocks)]
        for r in range(blocks):
            at = slice(r * lanes, (r + 1) * lanes)
            rt, rm, rs = rowtag[ri, at, :], rowmax[ri, at, :], rowsum[ri, at, :]
            for k in range(blocks):
                v = jnp.where(rt == tag[k], s[at, k * lanes : (k + 1) * lanes], MASKED)
                e = jnp.exp(20.0 * v)
                rm, rs = jnp.maximum(rm, v), rs + e
                cm[k] = jnp.maximum(cm[k], jnp.max(v.reshape(lanes // 8, 8, lanes), axis=0))
                cs[k] = cs[k] + jnp.sum(e.reshape(lanes // 8, 8, lanes), axis=0)
            rowmax[ri, at, :], rowsum[ri, at, :] = rm, rs
        for k in range(blocks):
            colmax[j, :, k * lanes : (k + 1) * lanes] = cm[k]
            colsum[j, :, k * lanes : (k + 1) * lanes] = cs[k]

    def own_tile(a):
        s = scores(a, a)
        off = lax.broadcasted_iota(jnp.int32, (lanes, lanes), 0) != lax.broadcasted_iota(
            jnp.int32, (lanes, lanes), 1
        )
        for r in range(blocks):
            at = slice(r * lanes, (r + 1) * lanes)
            rt, rm, rs = rowtag[a, at, :], rowmax[a, at, :], rowsum[a, at, :]
            for k in range(blocks):
                hit = rt == ct[a, 0:1, k * lanes : (k + 1) * lanes]
                if r == k:
                    hit = hit & off
                v = jnp.where(hit, s[at, k * lanes : (k + 1) * lanes], MASKED)
                e = jnp.exp(20.0 * v)
                rm, rs = jnp.maximum(rm, v), rs + e
            rowmax[a, at, :], rowsum[a, at, :] = rm, rs

    events, selfs, count = {}, [], 0
    for s in plan:
        if s[0] == "ev":
            events.setdefault(count, []).append(s[1:])
        else:
            if s[0] == "self":
                selfs.append(count)
            count += 1

    def turn(t, carry):
        for when, what in events.items():

            @pl.when(t == when)
            def _(what=what):
                for kind, q in what:
                    event(kind, q)

        own = (t == selfs[0]) | (t == selfs[1])

        @pl.when(own)
        def _():
            own_tile(t // selfs[1])

        @pl.when(jnp.logical_not(own))
        def _():
            tile(*operands(t))

        return carry

    lax.fori_loop(0, count, turn, 0)

    def flat(ref, ri, k, op):
        return op(
            jnp.transpose(ref[ri, k * lanes : (k + 1) * lanes, :]), axis=0, keepdims=True
        )

    def collect(j):
        for a in (0, 1):
            top = jnp.max(colmax[2 * j + a], axis=0, keepdims=True)
            total = jnp.sum(colsum[2 * j + a], axis=0, keepdims=True)
            msg[2 * j + a, 0:1, :], msg[2 * j + a, 1:2, :] = top, total
            if j in ROWSLOT:
                ri = 2 * ROWSLOT[j] + a
                for k in range(blocks):
                    at = slice(k * lanes, (k + 1) * lanes)
                    msg[2 * j + a, 0:1, at] = jnp.maximum(
                        msg[2 * j + a, 0:1, at], flat(rowmax, ri, k, jnp.max)
                    )
                    msg[2 * j + a, 1:2, at] = msg[2 * j + a, 1:2, at] + flat(
                        rowsum, ri, k, jnp.sum
                    )

    def send_msg(j):
        return pltpu.make_async_remote_copy(
            msg.at[pl.ds(2 * j, 2)], rmsg.at[pl.ds(2 * j, 2)], m_s.at[j - 1], m_r.at[j - 1],
            device_id=owner[j], device_id_type=MESH,
        )

    for j in (3, 5, 2, 1, 4):
        collect(j)
        send_msg(j).start()
    collect(0)
    for j in range(1, SLOTS):
        landed(rmsg.at[pl.ds(2 * j, 2)], m_r.at[j - 1])
    for a in (0, 1):
        top, total = msg[a, 0:1, :], msg[a, 1:2, :]
        for j in range(1, SLOTS):
            top = jnp.maximum(top, rmsg[2 * j + a, 0:1, :])
            total = total + rmsg[2 * j + a, 1:2, :]
        mass = jnp.log(1.0 + total)
        for k in range(4):
            res[4 * a + k, 0:1, 0:cap] = top[:, k * cap : (k + 1) * cap]
            res[4 * a + k, 1:2, 0:cap] = mass[:, k * cap : (k + 1) * cap]

    def send_back(q):
        ys = (y - ORDER[q // 2] + 4) % 4
        xs = x + c * (x3 - x)
        n = 2 * (q // 2) + c
        return pltpu.make_async_remote_copy(
            res.at[q], back.at[n], b_s.at[q], b_r.at[n],
            device_id=dev(xs, ys, z, q % 2), device_id_type=MESH,
        )

    keep_back = pltpu.make_async_copy(res.at[0], back.at[0], b_r.at[0])
    for q in range(GROUPS):
        start(q, send_back(q), keep_back)
    for n in range(GROUPS):
        landed(back.at[n], b_r.at[n])

    target8, rank8 = ids[0], ids[1]
    outs = [jnp.zeros((8, lanes), F32), jnp.zeros((8, lanes), F32)]
    for n in range(GROUPS):
        for k in (0, 1):
            line = jnp.broadcast_to(back[n, k : k + 1, :], (8, lanes))
            found = jnp.take_along_axis(line, rank8, axis=1)
            outs[k] = jnp.where(target8 == n, found, outs[k])
    best_ref[...] = outs[0][0 : rows // lanes]
    mass_ref[...] = outs[1][0 : rows // lanes]

    def left(ref, sem):
        pltpu.make_async_copy(ref, ref, sem).wait()

    for n in range(GROUPS):
        if n:
            send_tag(n).wait_send()
            send_rows(n).wait_send()
            send_back(n).wait_send()
        else:
            pl.when(c == 1)(send_tag(n).wait_send)
            pl.when(c == 1)(send_rows(n).wait_send)
            pl.when(c == 1)(send_back(n).wait_send)
    for j in range(1, SLOTS):
        send_ct(j).wait_send()
        send_msg(j).wait_send()
    for q in range(GROUPS):
        forward(0, 1, q, ahead).wait_send()
        forward(0, 4, q, sibling).wait_send()
        forward(1, 2, q, ahead).wait_send()
        forward(1, 5, q, sibling).wait_send()
        forward(0, 3, q, across).wait_send()


def body(embeddings, cluster_id, cluster_group):
    rows, width = embeddings.shape
    cap = rows * 3 // (2 * GROUPS)
    half, lanes = 4 * cap, 128
    dma = pltpu.SemaphoreType.DMA
    out = jax.ShapeDtypeStruct((rows // lanes, lanes), F32)
    best, mass = pl.pallas_call(
        functools.partial(kernel, cap),
        out_shape=(out, out),
        in_specs=[
            pl.BlockSpec(memory_space=pltpu.VMEM),
            pl.BlockSpec(memory_space=pltpu.SMEM),
            pl.BlockSpec(memory_space=pl.ANY),
        ],
        out_specs=(
            pl.BlockSpec(memory_space=pltpu.VMEM),
            pl.BlockSpec(memory_space=pltpu.VMEM),
        ),
        scratch_shapes=[
            pltpu.VMEM((rows, width), F32),
            pltpu.VMEM((rows, width), BF16),
            pltpu.VMEM((GROUPS * cap, rows), BF16),
            pltpu.VMEM((GROUPS * cap, width), BF16),
            pltpu.VMEM((2 * SLOTS, half, width), BF16),
            pltpu.VMEM((GROUPS, 8, lanes), F32),
            pltpu.VMEM((GROUPS, 8, lanes), F32),
            pltpu.VMEM((2 * SLOTS, 8, half), F32),
            pltpu.VMEM((6, half, lanes), F32),
            pltpu.VMEM((6, half, lanes), F32),
            pltpu.VMEM((6, half, lanes), F32),
            pltpu.VMEM((2 * SLOTS, 8, half), F32),
            pltpu.VMEM((2 * SLOTS, 8, half), F32),
            pltpu.VMEM((2 * SLOTS, 8, half), F32),
            pltpu.VMEM((2 * SLOTS, 8, half), F32),
            pltpu.VMEM((GROUPS, 8, lanes), F32),
            pltpu.VMEM((GROUPS, 8, lanes), F32),
            pltpu.VMEM((2, 8, lanes), jnp.int32),
            dma((4,)),
            dma((GROUPS,)), dma((GROUPS,)),
            dma((SLOTS - 1, GROUPS)), dma((SLOTS - 1, GROUPS)),
            dma((GROUPS,)), dma((GROUPS,)),
            dma((SLOTS - 1,)), dma((SLOTS - 1,)),
            dma((SLOTS - 1,)), dma((SLOTS - 1,)),
            dma((GROUPS,)), dma((GROUPS,)),
        ],
        compiler_params=pltpu.CompilerParams(
            collective_id=0, has_side_effects=True, vmem_limit_bytes=48 * 2**20
        ),
    )(cluster_id.reshape(1, rows), cluster_group, embeddings)
    return best.reshape(rows), mass.reshape(rows)


def solution(mesh):
    in_specs = (P(("grp", "blk"), None), P(("grp", "blk")), P())
    out_specs = (P(("grp", "blk")), P(("grp", "blk")))
    return jax.shard_map(body, mesh=mesh, in_specs=in_specs, out_specs=out_specs, check_vma=False)
```

time: 266 us -> 94.8 us (0.36)
  waiting for transfers between devices: 132 us -> 0 us
  Pallas kernels: 0 us -> 89.9 us
  blocking collectives: 48.6 us -> 0 us
  matrix products: 35.2 us -> 0 us
  between operations: 14.1 us -> 0.65 us
  starting transfers between devices: 13.1 us -> 0 us
  other arithmetic: 10 us -> 0 us
  local copies, waits for them, and re-layouts: 13 us -> 4.08 us
    all_gather x1 -> x0, waiting for transfers between devices: 120 us -> none  [body(): units_p = lax.all_gather(local, 'blk', axis=0, tiled=True)]
    pallas_call x0 -> x1, Pallas kernels: none -> 89.9 us  [body(): pl.pallas_call(functools.partial(kernel, cap), out_shape=(out, out), in_s...]
    dot_general x1 -> x0, matrix products: 35.2 us -> none  [pair_scores(): lax.dot_general(left, right, (((1,), (1,)), ((), ())), preferred_element_...]
    all_to_all x1 -> x0, blocking collectives: 26.6 us -> none  [body(): lax.all_to_all(outgoing.reshape(groups, capacity, width), 'grp', split_ax...]
    all_gather x1 -> x0, blocking collectives: 22 us -> none  [body(): tags_p = lax.all_gather(tags, 'blk', axis=0, tiled=True)]
    all_to_all x3 -> x0, starting transfers between devices: 13.1 us -> none  [the longest x1 4.96 us: body(): lax.all_to_all(mass.reshape(groups, capacity), 'grp', split_axis=0, conca...]
    all_to_all x3 -> x0, waiting for transfers between devices: 11.8 us -> none  [the longest x1 4.59 us: body(): lax.all_to_all(labels.reshape(groups, capacity), 'grp', split_axis=0, con...]
    gather x2 -> x0, local copies, waits for them, and re-layouts: 6.82 us -> none  [the longest x1 3.41 us: body(): log_mass = back_mass.reshape(-1)[slot]]
  transfers between devices with their start and end apart: 4 -> 0, of which waited for: 4 -> 0; matrix products, arithmetic and copies ran while one was open for 2% -> 0% of each run, Pallas kernels for 0% -> 0%
where the time goes in v1:
time: 94.8 us; the launch traced here: 94.6 us
  Pallas kernels  89.9 us (95%)
  local copies, waits for them, and re-layouts  4.08 us (4%)
    pallas_call x1, Pallas kernels, body(): pl.pallas_call(functools.partial(kernel, cap), out_shape=(out, out), in_s...  89.9 us
    unnamed x8, local copies, waits for them, and re-layouts  4.08 us

profile of v1, /device:TPU:1, one launch (start us, length us, event | category | flops | bytes accessed | tf_op | source)
XLA Modules:
  0.0 94.6 jit_solution(10498888383801931483)
XLA Ops:
  0.6 0.0 copy-start
  0.6 1.6 %copy-done = f32[512,1024]{1,0:T(8,128)S(1)} copy-done((f32[512,1024]{1,0:T(8,128)S(1)}, f32[512,1024]{1,0:T(8,128)}, u32[]{:S(2)}) %copy-start) | copy-done | bytes 2097176
  2.2 0.0 copy-start.1
  2.2 0.7 copy-done.1
  2.9 0.0 copy-start.2
  2.9 0.7 copy-done.2
  3.6 89.9 %shard_map.50 = (f32[4,128]{1,0:T(4,128)S(1)}, f32[4,128]{1,0:T(4,128)S(1)}) custom-call(s32[1,512]{1,0:T(1,128)S(1)} %bitcast.5, s32[64]{0:T(128)S(1)} %copy-done.2, f32[512,1024]{1,0:T(8,128)S(1)} %copy-done), custom_call_target="tpu_custom_call" | custom-call | tf_op jit(solution)/shard_map/pallas_call | solution.py:479
  93.4 0.6 copy.7
  94.0 0.6 copy.8
Async XLA Ops:
  0.6 1.6 %copy-start = (f32[512,1024]{1,0:T(8,128)S(1)}, f32[512,1024]{1,0:T(8,128)}, u32[]{:S(2)}) copy-start(f32[512,1024]{1,0:T(8,128)} %emb_ref.1) | copy-start | bytes 6291460
  2.2 0.7 copy-start.1
  2.9 0.7 copy-start.2

commit v2 on v1

--- a/solution.py
+++ b/solution.py
@@ -13,69 +13,38 @@
 GROUPS = 8
 SLOTS = 6
 MASKED = -30.0
-ORDER = (0, 1, 3, 2)
-
-ZB, XB, CB = "z", "x", "c"
-
-
-def program():
-    steps = []
-
-    def ev(*names):
-        steps.extend(("ev", kind, q) for kind, qs in names for q in qs)
-
-    def full(i, a, j, b):
-        steps.append(("tile", i, a, j, b))
-
-    def self_tile(a):
-        steps.append(("self", a))
-
-    ev(("E0", [0, 1]), ("E1", [0, 1]), ("E0", [2, 3]))
-    self_tile(0)
-    ev(("E1", [2]), ("E2", [0]), ("E0", [4, 5]), ("E2", [1]), ("E1", [3]))
-    full(0, 0, 1, 0)
-    ev(("E4", [0, 1, 2, 3]), ("E2", [2]), ("E1", [4]))
-    ev(("E2", [3]), ("E1", [5]), ("E3", [0, 1, 2, 3]))
-    full(3, 0, 1, 0)
-    ev(("E2", [4]), ("E5", [0, 1, 2, 3]))
-    full(3, 0, 4, 0)
-    ev(("E2", [5]), ("E0", [6]))
-    full(3, 0, 5, 0)
-    ev(("E0", [7]), ("E1", [6]))
-    self_tile(1)
-    full(0, 0, 0, 1)
-    ev(("E1", [7]), ("E2", [6]))
-    full(0, 1, 1, 0)
-    full(0, 1, 2, 0)
-    ev(("E2", [7]))
-    full(0, 1, 3, 0)
-    full(0, 1, 5, 0)
-    full(0, 1, 4, 0)
-    ev(("E4", [4, 5, 6, 7]))
-    full(0, 0, 1, 1)
-    full(0, 1, 1, 1)
-    full(3, 0, 1, 1)
-    full(3, 0, 4, 1)
-    full(0, CB, 4, CB)
-    full(5, 0, 1, 1)
-    ev(("E5", [4, 5, 6, 7]))
-    full(0, ZB, 2, ZB)
-    full(3, 0, 2, 1)
-    full(3, 0, 5, 1)
-    full(0, CB, 5, CB)
-    full(5, 0, 2, 1)
-    full(5, CB, 2, CB)
-    full(5, CB, 1, CB)
-    ev(("E3", [4, 5, 6, 7]))
-    full(3, 1, 1, 0)
-    full(3, 1, 1, 1)
-    full(0, XB, 3, XB)
-    full(3, XB, 2, XB)
-    full(3, 1, 5, 0)
-    full(3, 1, 5, 1)
-    full(3, 1, 4, 0)
-    full(3, 1, 4, 1)
-    return steps
+SENDS = ((0, 0), (0, 1), (1, 0), (3, 0), (1, 1), (3, 1), (2, 0), (2, 1))
+
+KINDS = {"n": 0, "w": 1, "s": 2}
+SLOT_OF = {"E": 0, "F": 1, "G": 2, "K": 3, "D": 4, "H": 5}
+PROGRAMS = (
+    (
+        "S1", "S2", "E0", "W2", "S3", "T0", "E2", "F0", "W1", "S4", "W3", "S6", "E1", "E3", "R0",
+        ("s", 0, 0, 0, 0), "C4", "D0", "D1", "D2", "D3", ("n", 0, 0, 4, 0), "W4", "S5", "F2", "G0", "E4", "C3",
+        "K0", "K1", "K2", "K3", "R3", ("n", 3, 0, 4, 0), "E6", "F1", "F3", "C1", ("n", 0, 0, 1, 0),
+        ("n", 3, 0, 1, 0), "W5", "S7", "C5", "H0", "H1", "H2", "H3", ("n", 3, 0, 5, 0), ("n", 0, 0, 5, 0),
+        "E5", "R5", ("n", 5, 0, 1, 0), "G2", "E7", ("s", 0, 1, 0, 1), "F4", ("n", 0, 0, 0, 1),
+        ("n", 0, 1, 1, 0), "D4", "D5", "D6", "D7", ("n", 3, 0, 4, 1), ("n", 0, 1, 3, 0), "F6", "G1",
+        ("n", 0, 1, 5, 0), "G3", "C2", ("n", 0, 1, 2, 0), ("n", 0, 1, 4, 0), "K4", "K5", "K6", "K7",
+        ("w", 3, 1, 4, 0), "F5", ("n", 0, "x", 3, "x"), ("n", 5, 0, 2, 0), "F7", ("n", 0, 0, 1, 1), "G4",
+        ("n", 0, 1, 1, 1), ("n", 3, 0, 1, 1), "G6", ("w", 3, 1, 1, 0), "H4", "H5", "H6", "H7",
+        ("n", 3, 0, 5, 1), "G5", ("w", 3, 1, 5, 0), ("n", 5, 0, 1, 1), "G7", ("n", 0, "z", 2, "z"),
+        ("n", 3, 0, 2, 1), ("n", 3, "x", 2, "x"), ("n", 5, 0, 2, 1),
+    ),
+    (
+        "S1", "S3", "E0", "W3", "S2", "T0", "E3", "F0", "W1", "S5", "W2", "S6", "E1", "E2", "R0",
+        ("s", 0, 0, 0, 0), "W5", "S4", "F3", "G0", "E5", "E6", "F1", "F2", "C1", ("n", 0, 0, 1, 0), "W4", "S7",
+        "E4", "G3", "E7", ("s", 0, 1, 0, 1), "F5", ("n", 0, 0, 0, 1), ("n", 0, 1, 1, 0), "C5", "H0", "H1",
+        "H2", "H3", ("n", 0, 1, 5, 0), "C4", "D0", "D1", "D2", "D3", ("n", 0, 1, 4, 0), "F6", "G1", "D4", "D5",
+        "D6", "D7", ("n", 0, 1, 4, 1), "G2", "C2", ("n", 0, 1, 2, 0), "F4", "F7", ("n", 0, 0, 1, 1), "G5",
+        ("n", 0, 1, 1, 1), "C3", "K0", "K1", "K2", "K3", "R3", ("n", 3, 0, 1, 0), "G6", ("n", 3, 0, 1, 1),
+        ("n", 3, 0, 5, 0), "G4", "H4", "H5", "H6", "H7", ("n", 3, 0, 5, 1), ("n", 3, 0, 4, 0), "G7",
+        ("n", 3, 0, 4, 1), ("n", 0, "z", 2, "z"), ("n", 0, 1, 3, 0), ("n", 3, 0, 2, 1), ("n", 0, 1, 5, 1),
+        "R5", ("n", 5, 0, 2, 1), ("n", 5, 1, 2, 1), ("n", 5, 0, 1, 1), ("n", 5, 1, 1, 1), "K4", "K5", "K6",
+        "K7", ("w", 3, 1, 1, 0), ("w", 3, 1, 5, 0), ("w", 3, 1, 4, 0), ("n", 0, "x", 3, "x"),
+        ("n", 3, "x", 2, "x"),
+    ),
+)
 
 
 ROWSLOT = {0: 0, 3: 1, 5: 2}
@@ -115,11 +84,9 @@
     barrier = pltpu.get_barrier_semaphore()
     friends = []
     for dy in range(4):
-        yd = (y + dy) % 4
-        for pc in (0, 1):
-            if dy:
-                friends.append(dev(x, yd, z, pc))
-            friends.append(dev(x3, yd, z, pc))
+        if dy:
+            friends.append(dev(x, (y + dy) % 4, z, c))
+        friends.append(dev(x3, (y + dy) % 4, z, c))
     friends += [
         dev(x, y, z, 1 - c), dev(x, y, zf, c), dev(x, y, zb, c), dev(x, y, z2, c),
         dev(xn, y, z, c), dev(xn, y, z2, c), dev(x, y, zf, 1 - c),
@@ -138,31 +105,57 @@
     for k in range(parts):
         load(k).start()
 
-    plan = program()
-    tiles = [s for s in plan if s[0] != "ev"]
-    bits = {ZB: z // 2, XB: xb, CB: c}
-
-    def pick(t, values):
-        value = 0
-        for k, (base, bit) in enumerate(values):
-            value = jnp.where(t == k, base + (bits[bit] if bit in bits else bit), value)
-        return value
+    events, tiles = [], []
+    for plan in PROGRAMS:
+        when, work = {}, []
+        for item in plan:
+            if isinstance(item, str):
+                when.setdefault(len(work), []).append((item[0], int(item[1])))
+            else:
+                work.append(item)
+        events.append(when)
+        tiles.append(work)
+    count = len(tiles[0])
+    bits = {"z": z // 2, "x": xb}
+
+    def number(item):
+        kind, i, a, j, b = item
+        base = 256 * KINDS[kind] + 16 * (2 * j) + 2 * i
+        if a in bits:
+            return base, a
+        return base + a + 16 * b, None
+
+    words = []
+    for k in range(0, count, 3):
+        both = []
+        for work in tiles:
+            word = 0
+            for r, item in enumerate(work[k : k + 3]):
+                base, bit = number(item)
+                word = word + base * 1024**r
+                if bit is not None:
+                    word = word + bits[bit] * (17 * 1024**r)
+            both.append(word)
+        words.append(jnp.where(c == 0, both[0], both[1]))
 
     def operands(t):
-        work = [s[1:] if s[0] == "tile" else (0, 0, 0, 0) for s in tiles]
-        ri = pick(t, [(2 * ROWSLOT[i], a) for i, a, _, _ in work])
-        i = ri + jnp.where(ri < 2, 0, jnp.where(ri < 4, 4, 6))
-        j = pick(t, [(2 * j, a) for _, _, j, a in work])
-        return ri, i, j
+        u, r = t // 3, t % 3
+        word = words[0]
+        for k in range(1, len(words)):
+            word = jnp.where(u == k, words[k], word)
+        code = jnp.where(r == 0, word, jnp.where(r == 1, word // 1024, word // 1024**2)) % 1024
+        kind, j, i = code // 256, code // 16 % 16, code % 16
+        return kind, i - jnp.where(i < 2, 0, jnp.where(i < 8, 4, 6)), i, j
 
     cid = cid_ref[...]
     group = jnp.zeros(cid.shape, jnp.int32)
     for k in range(cg_ref.shape[0]):
         group = jnp.where(cid == k, cg_ref[k], group)
     dy = ((group >> 1) - y) & 3
-    order = jnp.where(dy == 0, 0, jnp.where(dy == 1, 1, jnp.where(dy == 3, 2, 3)))
-    other = jnp.where((group & 1) == h, 0, 1)
-    target = 2 * order + other
+    other = (group & 1) ^ h
+    target = jnp.zeros(cid.shape, jnp.int32)
+    for n, (sy, sx) in enumerate(SENDS):
+        target = jnp.where((dy == sy) & (other == sx), n, target)
     picks = jnp.where(
         lax.broadcasted_iota(jnp.int32, (GROUPS, rows), 0) == target, 1.0, 0.0
     ).astype(F32)
@@ -198,63 +191,40 @@
     res[...] = jnp.zeros(res.shape, F32)
     msg[...] = jnp.zeros(msg.shape, F32)
 
-    pl.semaphore_wait(barrier, len(friends))
-
-    def chunk(slot, q):
-        return sh.at[2 * slot + q // 4, pl.ds((q % 4) * cap, cap)]
-
-    def dest(n):
-        yd = (y + ORDER[n // 2]) % 4
-        return dev(x, yd, z, 0) if n % 2 == 0 else dev(x3, yd, z, 1)
-
-    def landing(n):
-        q = 2 * (n // 2) + c
-        return sh.at[(n // 2) // 2, pl.ds((2 * ((n // 2) % 2) + c) * cap, cap)], q
-
-    def send_tag(n):
-        q = 2 * (n // 2) + c
-        return pltpu.make_async_remote_copy(
-            tagout.at[n], tagin.at[q], t_s.at[n], t_r.at[q], device_id=dest(n), device_id_type=MESH
-        )
-
-    def send_rows(n):
-        dst, q = landing(n)
-        return pltpu.make_async_remote_copy(
-            outgo.at[pl.ds(n * cap, cap)], dst, a_s.at[n], a_r.at[q],
-            device_id=dest(n), device_id_type=MESH,
-        )
-
-    keep_tag = pltpu.make_async_copy(tagout.at[0], tagin.at[0], t_r.at[0])
-    keep_rows = pltpu.make_async_copy(outgo.at[pl.ds(0, cap)], chunk(0, 0), a_r.at[0])
-
-    def start(n, remote, local):
-        if n:
-            remote.start()
-        else:
-            pl.when(c == 0)(local.start)
-            pl.when(c == 1)(remote.start)
-
-    for n in range(GROUPS):
-        start(n, send_tag(n), keep_tag)
-
     for k in range(parts):
         load(k).wait()
         v = emb[pl.ds(k * size, size)]
         scale = lax.rsqrt(jnp.sum(v * v, axis=1, keepdims=True) + 1e-06)
         unit[pl.ds(k * size, size)] = (v * scale).astype(BF16)
-    for k in range(GROUPS // 2):
-        outgo[pl.ds(2 * k * cap, 2 * cap)] = jnp.dot(
-            hot[pl.ds(2 * k * cap, 2 * cap)], unit[...], preferred_element_type=F32
-        ).astype(BF16)
-        for n in (2 * k, 2 * k + 1):
-            start(n, send_rows(n), keep_rows)
+    packed = jnp.dot(hot[...], unit[...], preferred_element_type=F32).astype(BF16)
+    sh[0, 0:cap] = packed[0:cap]
+    outgo[...] = packed
+
+    pl.semaphore_wait(barrier, len(friends))
+
+    def chunk(slot, q):
+        return sh.at[2 * slot + q // 4, pl.ds((q % 4) * cap, cap)]
+
+    def dest(n):
+        sy, sx = SENDS[n]
+        return dev(x3 if sx else x, (y + sy) % 4, z, c)
+
+    def send_tag(n):
+        return pltpu.make_async_remote_copy(
+            tagout.at[n], tagin.at[n], t_s.at[n], t_r.at[n], device_id=dest(n), device_id_type=MESH
+        )
+
+    def send_rows(n):
+        return pltpu.make_async_remote_copy(
+            outgo.at[pl.ds(n * cap, cap)], chunk(0, n), a_s.at[n], a_r.at[n],
+            device_id=dest(n), device_id_type=MESH,
+        )
+
+    for n in range(1, GROUPS):
+        send_tag(n).start()
 
     def landed(ref, sem):
         pltpu.make_async_copy(ref, ref, sem).wait()
-
-    for q in range(GROUPS):
-        landed(tagin.at[q], t_r.at[q])
-        ct[q // 4, :, (q % 4) * cap : (q % 4 + 1) * cap] = tagin[q, :, 0:cap]
 
     def send_ct(j):
         return pltpu.make_async_remote_copy(
@@ -262,8 +232,14 @@
             device_id=holder[j], device_id_type=MESH,
         )
 
-    for j in range(1, SLOTS):
-        send_ct(j).start()
+    def own_tags():
+        for q in range(GROUPS):
+            if q:
+                landed(tagin.at[q], t_r.at[q])
+            tag = tagin if q else tagout
+            ct[q // 4, :, (q % 4) * cap : (q % 4 + 1) * cap] = tag[q, :, 0:cap]
+        for j in range(1, SLOTS):
+            send_ct(j).start()
 
     def row_tags(slot):
         for a in (0, 1):
@@ -274,12 +250,6 @@
                     jnp.broadcast_to(v, (lanes, lanes))
                 )
 
-    row_tags(0)
-    for j in range(1, SLOTS):
-        landed(ct.at[pl.ds(2 * j, 2)], ct_r.at[j - 1])
-    row_tags(3)
-    row_tags(5)
-
     def forward(src, slot, q, to):
         return pltpu.make_async_remote_copy(
             chunk(src, q), chunk(slot, q), f_s.at[slot - 1, q], f_r.at[slot - 1, q],
@@ -289,9 +259,20 @@
     ahead, across, sibling = dev(x, y, zf, c), dev(xn, y, z, c), dev(x, y, z, 1 - c)
 
     def event(kind, q):
-        slot = int(kind[1])
+        if kind == "T":
+            return own_tags()
+        if kind == "R":
+            return row_tags(q)
+        if kind == "C":
+            return landed(ct.at[pl.ds(2 * q, 2)], ct_r.at[q - 1])
+        if kind == "S":
+            return send_rows(q).start()
+        if kind == "W":
+            return send_rows(q).wait_send()
+        slot = SLOT_OF[kind]
         sem = a_r.at[q] if slot == 0 else f_r.at[slot - 1, q]
-        landed(chunk(slot, q), sem)
+        if slot or q:
+            landed(chunk(slot, q), sem)
         if slot == 0:
             forward(0, 1, q, ahead).start()
             pl.when(c == 0)(forward(0, 3, q, across).start)
@@ -309,30 +290,30 @@
 
     def scores(i, j):
         return lax.dot_general(
-            sh[i], sh[j], (((1,), (1,)), ((), ())), preferred_element_type=F32
-        )
-
-    def tile(ri, i, j):
-        s = scores(i, j)
-        cm = [colmax[j, :, k * lanes : (k + 1) * lanes] for k in range(blocks)]
-        cs = [colsum[j, :, k * lanes : (k + 1) * lanes] for k in range(blocks)]
-        tag = [ct[j, 0:1, k * lanes : (k + 1) * lanes] for k in range(blocks)]
+            sh[i], j, (((1,), (1,)), ((), ())), preferred_element_type=F32
+        )
+
+    def tile(ri, i, j, halves):
+        s = scores(i, sh[pl.ds(j, halves)].reshape(halves * half, width))
+        cols = [(j + a, slice(k * lanes, (k + 1) * lanes)) for a in range(halves) for k in range(blocks)]
+        cm = [colmax[n, :, at] for n, at in cols]
+        cs = [colsum[n, :, at] for n, at in cols]
+        tag = [ct[n, 0:1, at] for n, at in cols]
         for r in range(blocks):
             at = slice(r * lanes, (r + 1) * lanes)
             rt, rm, rs = rowtag[ri, at, :], rowmax[ri, at, :], rowsum[ri, at, :]
-            for k in range(blocks):
+            for k in range(len(cols)):
                 v = jnp.where(rt == tag[k], s[at, k * lanes : (k + 1) * lanes], MASKED)
                 e = jnp.exp(20.0 * v)
                 rm, rs = jnp.maximum(rm, v), rs + e
                 cm[k] = jnp.maximum(cm[k], jnp.max(v.reshape(lanes // 8, 8, lanes), axis=0))
                 cs[k] = cs[k] + jnp.sum(e.reshape(lanes // 8, 8, lanes), axis=0)
             rowmax[ri, at, :], rowsum[ri, at, :] = rm, rs
-        for k in range(blocks):
-            colmax[j, :, k * lanes : (k + 1) * lanes] = cm[k]
-            colsum[j, :, k * lanes : (k + 1) * lanes] = cs[k]
+        for k, (n, at) in enumerate(cols):
+            colmax[n, :, at], colsum[n, :, at] = cm[k], cs[k]
 
     def own_tile(a):
-        s = scores(a, a)
+        s = scores(a, sh[a])
         off = lax.broadcasted_iota(jnp.int32, (lanes, lanes), 0) != lax.broadcasted_iota(
             jnp.int32, (lanes, lanes), 1
         )
@@ -348,32 +329,36 @@
                 rm, rs = jnp.maximum(rm, v), rs + e
             rowmax[a, at, :], rowsum[a, at, :] = rm, rs
 
-    events, selfs, count = {}, [], 0
-    for s in plan:
-        if s[0] == "ev":
-            events.setdefault(count, []).append(s[1:])
-        else:
-            if s[0] == "self":
-                selfs.append(count)
-            count += 1
+    group_of = 6
 
     def turn(t, carry):
-        for when, what in events.items():
-
-            @pl.when(t == when)
-            def _(what=what):
-                for kind, q in what:
-                    event(kind, q)
-
-        own = (t == selfs[0]) | (t == selfs[1])
-
-        @pl.when(own)
+        for first in range(0, count, group_of):
+
+            @pl.when(t // group_of == first // group_of)
+            def _(first=first):
+                for k in range(first, min(first + group_of, count)):
+                    for core in (0, 1):
+                        what = events[core].get(k, [])
+                        if what:
+
+                            @pl.when((t == k) & (c == core))
+                            def _(what=what):
+                                for kind, q in what:
+                                    event(kind, q)
+
+        kind, ri, i, j = operands(t)
+
+        @pl.when(kind == 0)
         def _():
-            own_tile(t // selfs[1])
-
-        @pl.when(jnp.logical_not(own))
+            tile(ri, i, j, 1)
+
+        @pl.when(kind == 1)
         def _():
-            tile(*operands(t))
+            tile(ri, i, j, 2)
+
+        @pl.when(kind == 2)
+        def _():
+            own_tile(ri)
 
         return carry
 
@@ -423,42 +408,33 @@
             res[4 * a + k, 1:2, 0:cap] = mass[:, k * cap : (k + 1) * cap]
 
     def send_back(q):
-        ys = (y - ORDER[q // 2] + 4) % 4
-        xs = x + c * (x3 - x)
-        n = 2 * (q // 2) + c
+        sy, sx = SENDS[q]
         return pltpu.make_async_remote_copy(
-            res.at[q], back.at[n], b_s.at[q], b_r.at[n],
-            device_id=dev(xs, ys, z, q % 2), device_id_type=MESH,
-        )
-
-    keep_back = pltpu.make_async_copy(res.at[0], back.at[0], b_r.at[0])
-    for q in range(GROUPS):
-        start(q, send_back(q), keep_back)
-    for n in range(GROUPS):
+            res.at[q], back.at[q], b_s.at[q], b_r.at[q],
+            device_id=dev(x3 if sx else x, (y - sy + 4) % 4, z, c), device_id_type=MESH,
+        )
+
+    for q in range(1, GROUPS):
+        send_back(q).start()
+    for n in range(1, GROUPS):
         landed(back.at[n], b_r.at[n])
 
     target8, rank8 = ids[0], ids[1]
     outs = [jnp.zeros((8, lanes), F32), jnp.zeros((8, lanes), F32)]
     for n in range(GROUPS):
         for k in (0, 1):
-            line = jnp.broadcast_to(back[n, k : k + 1, :], (8, lanes))
+            line = jnp.broadcast_to((back if n else res)[n, k : k + 1, :], (8, lanes))
             found = jnp.take_along_axis(line, rank8, axis=1)
             outs[k] = jnp.where(target8 == n, found, outs[k])
     best_ref[...] = outs[0][0 : rows // lanes]
     mass_ref[...] = outs[1][0 : rows // lanes]
 
-    def left(ref, sem):
-        pltpu.make_async_copy(ref, ref, sem).wait()
-
-    for n in range(GROUPS):
-        if n:
-            send_tag(n).wait_send()
-            send_rows(n).wait_send()
-            send_back(n).wait_send()
-        else:
-            pl.when(c == 1)(send_tag(n).wait_send)
-            pl.when(c == 1)(send_rows(n).wait_send)
-            pl.when(c == 1)(send_back(n).wait_send)
+    for n in range(1, GROUPS):
+        send_tag(n).wait_send()
+        send_back(n).wait_send()
+        for core in (0, 1):
+            if ("W", n) not in sum(events[core].values(), []):
+                pl.when(c == core)(send_rows(n).wait_send)
     for j in range(1, SLOTS):
         send_ct(j).wait_send()
         send_msg(j).wait_send()
@@ -516,7 +492,7 @@
             dma((GROUPS,)), dma((GROUPS,)),
         ],
         compiler_params=pltpu.CompilerParams(
-            collective_id=0, has_side_effects=True, vmem_limit_bytes=48 * 2**20
+            collective_id=0, has_side_effects=True, vmem_limit_bytes=60 * 2**20
         ),
     )(cluster_id.reshape(1, rows), cluster_group, embeddings)
     return best.reshape(rows), mass.reshape(rows)

time: 94.8 us -> 75.6 us (0.80)
  Pallas kernels: 89.9 us -> 72.2 us
  local copies, waits for them, and re-layouts: 4.08 us -> 2.48 us
    pallas_call x1, Pallas kernels: 89.9 us -> 72.2 us  [body(): pl.pallas_call(functools.partial(kernel, cap), out_shape=(out, out), in_s...]
    unnamed x8 -> x2, local copies, waits for them, and re-layouts: 4.08 us -> 2.48 us
where the time goes in v2:
time: 75.6 us; the launch traced here: 75.3 us
  Pallas kernels  72.2 us (96%)
  local copies, waits for them, and re-layouts  2.48 us (3%)
    pallas_call x1, Pallas kernels, body(): pl.pallas_call(functools.partial(kernel, cap), out_shape=(out, out), in_s...  72.2 us
    unnamed x2, local copies, waits for them, and re-layouts  2.48 us

profile of v2, /device:TPU:1, one launch (start us, length us, event | category | flops | bytes accessed | tf_op | source)
XLA Modules:
  0.0 75.3 jit_solution(16013789778397206732)
XLA Ops:
  0.6 72.2 %shard_map.50 = (f32[4,128]{1,0:T(4,128)}, f32[4,128]{1,0:T(4,128)}) custom-call(s32[1,512]{1,0:T(1,128)} %bitcast.5, s32[64]{0:T(128)} %cg_ref.1, f32[512,1024]{1,0:T(8,128)} %emb_ref.1), custom_call_target="tpu_custom_call" | custom-call | tf_op jit(solution)/shard_map/pallas_call | solution.py:455
  72.8 1.2 %copy.7 = f32[512]{0:T(512)} copy(f32[512]{0:T(512)} %bitcast.4) | data formatting | bytes 4096
  74.1 1.2 %copy.8 = f32[512]{0:T(512)} copy(f32[512]{0:T(512)} %bitcast.3) | data formatting | bytes 4096

commit v3 on v2

--- a/solution.py
+++ b/solution.py
@@ -19,30 +19,30 @@
 SLOT_OF = {"E": 0, "F": 1, "G": 2, "K": 3, "D": 4, "H": 5}
 PROGRAMS = (
     (
-        "S1", "S2", "E0", "W2", "S3", "T0", "E2", "F0", "W1", "S4", "W3", "S6", "E1", "E3", "R0",
-        ("s", 0, 0, 0, 0), "C4", "D0", "D1", "D2", "D3", ("n", 0, 0, 4, 0), "W4", "S5", "F2", "G0", "E4", "C3",
-        "K0", "K1", "K2", "K3", "R3", ("n", 3, 0, 4, 0), "E6", "F1", "F3", "C1", ("n", 0, 0, 1, 0),
-        ("n", 3, 0, 1, 0), "W5", "S7", "C5", "H0", "H1", "H2", "H3", ("n", 3, 0, 5, 0), ("n", 0, 0, 5, 0),
-        "E5", "R5", ("n", 5, 0, 1, 0), "G2", "E7", ("s", 0, 1, 0, 1), "F4", ("n", 0, 0, 0, 1),
-        ("n", 0, 1, 1, 0), "D4", "D5", "D6", "D7", ("n", 3, 0, 4, 1), ("n", 0, 1, 3, 0), "F6", "G1",
-        ("n", 0, 1, 5, 0), "G3", "C2", ("n", 0, 1, 2, 0), ("n", 0, 1, 4, 0), "K4", "K5", "K6", "K7",
-        ("w", 3, 1, 4, 0), "F5", ("n", 0, "x", 3, "x"), ("n", 5, 0, 2, 0), "F7", ("n", 0, 0, 1, 1), "G4",
-        ("n", 0, 1, 1, 1), ("n", 3, 0, 1, 1), "G6", ("w", 3, 1, 1, 0), "H4", "H5", "H6", "H7",
-        ("n", 3, 0, 5, 1), "G5", ("w", 3, 1, 5, 0), ("n", 5, 0, 1, 1), "G7", ("n", 0, "z", 2, "z"),
-        ("n", 3, 0, 2, 1), ("n", 3, "x", 2, "x"), ("n", 5, 0, 2, 1),
+        "S1", "S2", "S3", "E0", "T0", "F0", "W1", "W2", "W3", "S4", "S5", "E1", "E2", "E3", "R0",
+        ("s", 0, 0, 0, 0), "C4", "D0", "D1", "D2", "D3", ("n", 0, 0, 4, 0), "W4", "W5", "S6", "S7", "F1", "F2",
+        "F3", "C1", ("n", 0, 0, 1, 0), "E4", "E5", "C3", "K0", "K1", "K2", "K3", "R3", ("n", 3, 0, 1, 0), "C5",
+        "H0", "H1", "H2", "H3", ("n", 3, 0, 5, 0), ("n", 3, 0, 4, 0), ("n", 0, 0, 5, 0), "R5",
+        ("n", 5, 0, 1, 0), "E6", "E7", ("s", 0, 1, 0, 1), ("n", 0, 0, 0, 1), ("n", 0, 1, 1, 0), "D4", "D5",
+        "D6", "D7", ("n", 3, 0, 4, 1), "F4", "F5", "C2", "G0", "G1", "G2", "G3", ("n", 0, 1, 2, 0),
+        ("n", 0, 1, 3, 0), ("n", 0, 1, 5, 0), ("n", 0, 1, 4, 0), ("n", 5, 0, 2, 0), "F6", "F7",
+        ("n", 0, 0, 1, 1), ("n", 0, 1, 1, 1), ("n", 3, 0, 1, 1), "K4", "K5", "K6", "K7", ("w", 3, 1, 1, 0),
+        "H4", "H5", "H6", "H7", ("n", 3, 0, 5, 1), ("w", 3, 1, 5, 0), ("w", 3, 1, 4, 0), ("n", 0, "x", 3, "x"),
+        ("n", 5, 0, 1, 1), "G4", "G5", "G6", "G7", ("n", 0, "z", 2, "z"), ("n", 3, 0, 2, 1),
+        ("n", 3, "x", 2, "x"), ("n", 5, 0, 2, 1),
     ),
     (
-        "S1", "S3", "E0", "W3", "S2", "T0", "E3", "F0", "W1", "S5", "W2", "S6", "E1", "E2", "R0",
-        ("s", 0, 0, 0, 0), "W5", "S4", "F3", "G0", "E5", "E6", "F1", "F2", "C1", ("n", 0, 0, 1, 0), "W4", "S7",
-        "E4", "G3", "E7", ("s", 0, 1, 0, 1), "F5", ("n", 0, 0, 0, 1), ("n", 0, 1, 1, 0), "C5", "H0", "H1",
-        "H2", "H3", ("n", 0, 1, 5, 0), "C4", "D0", "D1", "D2", "D3", ("n", 0, 1, 4, 0), "F6", "G1", "D4", "D5",
-        "D6", "D7", ("n", 0, 1, 4, 1), "G2", "C2", ("n", 0, 1, 2, 0), "F4", "F7", ("n", 0, 0, 1, 1), "G5",
-        ("n", 0, 1, 1, 1), "C3", "K0", "K1", "K2", "K3", "R3", ("n", 3, 0, 1, 0), "G6", ("n", 3, 0, 1, 1),
-        ("n", 3, 0, 5, 0), "G4", "H4", "H5", "H6", "H7", ("n", 3, 0, 5, 1), ("n", 3, 0, 4, 0), "G7",
-        ("n", 3, 0, 4, 1), ("n", 0, "z", 2, "z"), ("n", 0, 1, 3, 0), ("n", 3, 0, 2, 1), ("n", 0, 1, 5, 1),
-        "R5", ("n", 5, 0, 2, 1), ("n", 5, 1, 2, 1), ("n", 5, 0, 1, 1), ("n", 5, 1, 1, 1), "K4", "K5", "K6",
-        "K7", ("w", 3, 1, 1, 0), ("w", 3, 1, 5, 0), ("w", 3, 1, 4, 0), ("n", 0, "x", 3, "x"),
-        ("n", 3, "x", 2, "x"),
+        "S1", "S2", "S3", "E0", "T0", "F0", "W1", "W2", "W3", "S4", "S5", "E1", "E2", "E3", "R0",
+        ("s", 0, 0, 0, 0), "G0", "W4", "W5", "S6", "S7", "F1", "F2", "F3", "C1", ("n", 0, 0, 1, 0), "E4", "E5",
+        "E6", "E7", ("s", 0, 1, 0, 1), ("n", 0, 0, 0, 1), "G1", "G2", "G3", ("n", 0, 1, 1, 0), "C2",
+        ("n", 0, 1, 2, 0), "F4", "F5", "C5", "H0", "H1", "H2", "H3", ("n", 0, 1, 5, 0), "C4", "D0", "D1", "D2",
+        "D3", ("n", 0, 1, 4, 0), "D4", "D5", "D6", "D7", ("n", 0, 1, 4, 1), "F6", "F7", ("n", 0, 0, 1, 1),
+        ("n", 0, 1, 1, 1), "R5", ("n", 5, 0, 1, 1), "H4", "H5", "H6", "H7", ("n", 0, 1, 5, 1),
+        ("n", 5, 1, 1, 1), "G4", "G5", "C3", "K0", "K1", "K2", "K3", "R3", ("n", 3, 0, 1, 0),
+        ("n", 3, 0, 1, 1), ("n", 3, 0, 5, 0), ("n", 3, 0, 5, 1), "G6", "G7", ("n", 3, 0, 4, 0),
+        ("n", 3, 0, 4, 1), ("n", 0, "z", 2, "z"), ("n", 0, 1, 3, 0), ("n", 3, 0, 2, 1), ("n", 5, 0, 2, 1),
+        ("n", 5, 1, 2, 1), "K4", "K5", "K6", "K7", ("w", 3, 1, 1, 0), ("w", 3, 1, 5, 0), ("w", 3, 1, 4, 0),
+        ("n", 0, "x", 3, "x"), ("n", 3, "x", 2, "x"),
     ),
 )
 
@@ -51,10 +51,10 @@
 
 
 def kernel(
-    cap, cid_ref, cg_ref, emb_ref, best_ref, mass_ref,
+    cap, cid_ref, cg_ref, emb_ref, out_ref,
     emb, unit, hot, outgo, sh, tagout, tagin, ct, rowtag,
-    rowmax, rowsum, colmax, colsum, msg, rmsg, res, back, ids,
-    in_sem, a_s, a_r, f_s, f_r, t_s, t_r, ct_s, ct_r, m_s, m_r, b_s, b_r,
+    rowmax, rowsum, colmax, colsum, part, back, ids,
+    in_sem, a_s, a_r, f_s, f_r, t_s, t_r, ct_s, ct_r, b_s, b_r,
 ):
     rows, width = emb.shape
     half = 4 * cap
@@ -188,8 +188,7 @@
     colmax[...] = jnp.full(colmax.shape, -1.0, F32)
     rowsum[...] = jnp.zeros(rowsum.shape, F32)
     colsum[...] = jnp.zeros(colsum.shape, F32)
-    res[...] = jnp.zeros(res.shape, F32)
-    msg[...] = jnp.zeros(msg.shape, F32)
+    part[...] = jnp.zeros(part.shape, F32)
 
     for k in range(parts):
         load(k).wait()
@@ -369,75 +368,60 @@
             jnp.transpose(ref[ri, k * lanes : (k + 1) * lanes, :]), axis=0, keepdims=True
         )
 
-    def collect(j):
+    places = {
+        0: (x, z, c), 1: (x, zb, c), 2: (x, z2, c), 3: (xn, z3, c), 4: (x, z, 1 - c), 5: (x, zf, 1 - c),
+    }
+
+    def send_part(j, q):
+        sy, sx = SENDS[q]
+        xo, zo, co = places[j]
+        return pltpu.make_async_remote_copy(
+            part.at[SLOTS * q + j], back.at[SLOTS * q + j], b_s, b_r,
+            device_id=dev(3 - xo if sx else xo, (y - sy + 4) % 4, zo, co), device_id_type=MESH,
+        )
+
+    for j in (4, 1, 2, 5, 3, 0):
         for a in (0, 1):
             top = jnp.max(colmax[2 * j + a], axis=0, keepdims=True)
             total = jnp.sum(colsum[2 * j + a], axis=0, keepdims=True)
-            msg[2 * j + a, 0:1, :], msg[2 * j + a, 1:2, :] = top, total
             if j in ROWSLOT:
                 ri = 2 * ROWSLOT[j] + a
-                for k in range(blocks):
-                    at = slice(k * lanes, (k + 1) * lanes)
-                    msg[2 * j + a, 0:1, at] = jnp.maximum(
-                        msg[2 * j + a, 0:1, at], flat(rowmax, ri, k, jnp.max)
-                    )
-                    msg[2 * j + a, 1:2, at] = msg[2 * j + a, 1:2, at] + flat(
-                        rowsum, ri, k, jnp.sum
-                    )
-
-    def send_msg(j):
-        return pltpu.make_async_remote_copy(
-            msg.at[pl.ds(2 * j, 2)], rmsg.at[pl.ds(2 * j, 2)], m_s.at[j - 1], m_r.at[j - 1],
-            device_id=owner[j], device_id_type=MESH,
-        )
-
-    for j in (3, 5, 2, 1, 4):
-        collect(j)
-        send_msg(j).start()
-    collect(0)
-    for j in range(1, SLOTS):
-        landed(rmsg.at[pl.ds(2 * j, 2)], m_r.at[j - 1])
-    for a in (0, 1):
-        top, total = msg[a, 0:1, :], msg[a, 1:2, :]
-        for j in range(1, SLOTS):
-            top = jnp.maximum(top, rmsg[2 * j + a, 0:1, :])
-            total = total + rmsg[2 * j + a, 1:2, :]
-        mass = jnp.log(1.0 + total)
-        for k in range(4):
-            res[4 * a + k, 0:1, 0:cap] = top[:, k * cap : (k + 1) * cap]
-            res[4 * a + k, 1:2, 0:cap] = mass[:, k * cap : (k + 1) * cap]
-
-    def send_back(q):
-        sy, sx = SENDS[q]
-        return pltpu.make_async_remote_copy(
-            res.at[q], back.at[q], b_s.at[q], b_r.at[q],
-            device_id=dev(x3 if sx else x, (y - sy + 4) % 4, z, c), device_id_type=MESH,
-        )
-
-    for q in range(1, GROUPS):
-        send_back(q).start()
-    for n in range(1, GROUPS):
-        landed(back.at[n], b_r.at[n])
+                top = jnp.maximum(
+                    top, jnp.concatenate([flat(rowmax, ri, k, jnp.max) for k in range(blocks)], axis=1)
+                )
+                total = total + jnp.concatenate(
+                    [flat(rowsum, ri, k, jnp.sum) for k in range(blocks)], axis=1
+                )
+            for k in range(4):
+                q = 4 * a + k
+                at = SLOTS * q + j
+                part[at, 0:1, 0:cap] = top[:, k * cap : (k + 1) * cap]
+                part[at, 1:2, 0:cap] = total[:, k * cap : (k + 1) * cap]
+                if at:
+                    send_part(j, q).start()
+    rest = pl.ds(1, SLOTS * GROUPS - 1)
+    landed(back.at[rest], b_r)
 
     target8, rank8 = ids[0], ids[1]
     outs = [jnp.zeros((8, lanes), F32), jnp.zeros((8, lanes), F32)]
     for n in range(GROUPS):
-        for k in (0, 1):
-            line = jnp.broadcast_to((back if n else res)[n, k : k + 1, :], (8, lanes))
-            found = jnp.take_along_axis(line, rank8, axis=1)
+        have = [(back if SLOTS * n + j else part)[SLOTS * n + j] for j in range(SLOTS)]
+        top = functools.reduce(jnp.maximum, have)[0:1]
+        mass = jnp.log(1.0 + functools.reduce(jnp.add, have)[1:2])
+        for k, line in enumerate((top, mass)):
+            found = jnp.take_along_axis(jnp.broadcast_to(line, (8, lanes)), rank8, axis=1)
             outs[k] = jnp.where(target8 == n, found, outs[k])
-    best_ref[...] = outs[0][0 : rows // lanes]
-    mass_ref[...] = outs[1][0 : rows // lanes]
+    for k in (0, 1):
+        out_ref[k * rows // lanes : (k + 1) * rows // lanes] = outs[k][0 : rows // lanes]
 
     for n in range(1, GROUPS):
         send_tag(n).wait_send()
-        send_back(n).wait_send()
         for core in (0, 1):
             if ("W", n) not in sum(events[core].values(), []):
                 pl.when(c == core)(send_rows(n).wait_send)
     for j in range(1, SLOTS):
         send_ct(j).wait_send()
-        send_msg(j).wait_send()
+    landed(part.at[rest], b_s)
     for q in range(GROUPS):
         forward(0, 1, q, ahead).wait_send()
         forward(0, 4, q, sibling).wait_send()
@@ -446,24 +430,26 @@
         forward(0, 3, q, across).wait_send()
 
 
+def part_in_two(both_ref, best_ref, mass_ref):
+    count = best_ref.shape[0]
+    best_ref[...] = both_ref[0:count]
+    mass_ref[...] = both_ref[count : 2 * count]
+
+
 def body(embeddings, cluster_id, cluster_group):
     rows, width = embeddings.shape
     cap = rows * 3 // (2 * GROUPS)
     half, lanes = 4 * cap, 128
     dma = pltpu.SemaphoreType.DMA
-    out = jax.ShapeDtypeStruct((rows // lanes, lanes), F32)
-    best, mass = pl.pallas_call(
+    both = pl.pallas_call(
         functools.partial(kernel, cap),
-        out_shape=(out, out),
+        out_shape=jax.ShapeDtypeStruct((2 * rows // lanes, lanes), F32),
         in_specs=[
             pl.BlockSpec(memory_space=pltpu.VMEM),
             pl.BlockSpec(memory_space=pltpu.SMEM),
             pl.BlockSpec(memory_space=pl.ANY),
         ],
-        out_specs=(
-            pl.BlockSpec(memory_space=pltpu.VMEM),
-            pl.BlockSpec(memory_space=pltpu.VMEM),
-        ),
+        out_specs=pl.BlockSpec(memory_space=pltpu.VMEM),
         scratch_shapes=[
             pltpu.VMEM((rows, width), F32),
             pltpu.VMEM((rows, width), BF16),
@@ -478,23 +464,22 @@
             pltpu.VMEM((6, half, lanes), F32),
             pltpu.VMEM((2 * SLOTS, 8, half), F32),
             pltpu.VMEM((2 * SLOTS, 8, half), F32),
-            pltpu.VMEM((2 * SLOTS, 8, half), F32),
-            pltpu.VMEM((2 * SLOTS, 8, half), F32),
-            pltpu.VMEM((GROUPS, 8, lanes), F32),
-            pltpu.VMEM((GROUPS, 8, lanes), F32),
+            pltpu.VMEM((SLOTS * GROUPS, 8, lanes), F32),
+            pltpu.VMEM((SLOTS * GROUPS, 8, lanes), F32),
             pltpu.VMEM((2, 8, lanes), jnp.int32),
             dma((4,)),
             dma((GROUPS,)), dma((GROUPS,)),
             dma((SLOTS - 1, GROUPS)), dma((SLOTS - 1, GROUPS)),
             dma((GROUPS,)), dma((GROUPS,)),
             dma((SLOTS - 1,)), dma((SLOTS - 1,)),
-            dma((SLOTS - 1,)), dma((SLOTS - 1,)),
-            dma((GROUPS,)), dma((GROUPS,)),
+            dma, dma,
         ],
         compiler_params=pltpu.CompilerParams(
             collective_id=0, has_side_effects=True, vmem_limit_bytes=60 * 2**20
         ),
     )(cluster_id.reshape(1, rows), cluster_group, embeddings)
+    one = jax.ShapeDtypeStruct((rows // lanes, lanes), F32)
+    best, mass = pl.pallas_call(part_in_two, out_shape=(one, one))(both)
     return best.reshape(rows), mass.reshape(rows)
 
 

time: 75.6 us -> 72.2 us (0.955)
  local copies, waits for them, and re-layouts: 2.48 us -> 0 us
  Pallas kernels: 72.2 us -> 71.4 us
    unnamed x2 -> x0, local copies, waits for them, and re-layouts: 2.48 us -> none
    pallas_call x1 -> x2, Pallas kernels: 72.2 us -> 71.4 us  [the longest x1 70.1 us: body(): pl.pallas_call(functools.partial(kernel, cap), out_shape=jax.ShapeDtypeSt...]
where the time goes in v3:
time: 72.2 us; the launch traced here: 72 us
  Pallas kernels  71.4 us (99%)
    pallas_call x1, Pallas kernels, body(): pl.pallas_call(functools.partial(kernel, cap), out_shape=jax.ShapeDtypeSt...  70.1 us

profile of v3, /device:TPU:1, one launch (start us, length us, event | category | flops | bytes accessed | tf_op | source)
XLA Modules:
  0.0 72.0 jit_solution(6974591617967277060)
XLA Ops:
  0.6 70.1 %shard_map.50.both_ref = f32[8,128]{1,0:T(8,128)} custom-call(s32[1,512]{1,0:T(1,128)} %bitcast.3, s32[64]{0:T(128)} %cg_ref.1, f32[512,1024]{1,0:T(8,128)} %emb_ref.1), custom_call_target="tpu_custom_call" | custom-call | tf_op jit(solution)/shard_map/pallas_call | solution.py:444
  70.7 1.3 %shard_map.51 = (f32[4,128]{1,0:T(4,128)}, f32[4,128]{1,0:T(4,128)}) custom-call(f32[8,128]{1,0:T(8,128)} %shard_map.50.both_ref), custom_call_target="tpu_custom_call" | custom-call | tf_op jit(solution)/shard_map/pallas_call | solution.py:482

commit v4 on v3

--- a/solution.py
+++ b/solution.py
@@ -15,45 +15,38 @@
 MASKED = -30.0
 SENDS = ((0, 0), (0, 1), (1, 0), (3, 0), (1, 1), (3, 1), (2, 0), (2, 1))
 
-KINDS = {"n": 0, "w": 1, "s": 2}
+KINDS = {"n": 0, "w": 1, "s": 2, "p": 3}
 SLOT_OF = {"E": 0, "F": 1, "G": 2, "K": 3, "D": 4, "H": 5}
 PROGRAMS = (
     (
-        "S1", "S2", "S3", "E0", "T0", "F0", "W1", "W2", "W3", "S4", "S5", "E1", "E2", "E3", "R0",
-        ("s", 0, 0, 0, 0), "C4", "D0", "D1", "D2", "D3", ("n", 0, 0, 4, 0), "W4", "W5", "S6", "S7", "F1", "F2",
-        "F3", "C1", ("n", 0, 0, 1, 0), "E4", "E5", "C3", "K0", "K1", "K2", "K3", "R3", ("n", 3, 0, 1, 0), "C5",
-        "H0", "H1", "H2", "H3", ("n", 3, 0, 5, 0), ("n", 3, 0, 4, 0), ("n", 0, 0, 5, 0), "R5",
-        ("n", 5, 0, 1, 0), "E6", "E7", ("s", 0, 1, 0, 1), ("n", 0, 0, 0, 1), ("n", 0, 1, 1, 0), "D4", "D5",
-        "D6", "D7", ("n", 3, 0, 4, 1), "F4", "F5", "C2", "G0", "G1", "G2", "G3", ("n", 0, 1, 2, 0),
-        ("n", 0, 1, 3, 0), ("n", 0, 1, 5, 0), ("n", 0, 1, 4, 0), ("n", 5, 0, 2, 0), "F6", "F7",
-        ("n", 0, 0, 1, 1), ("n", 0, 1, 1, 1), ("n", 3, 0, 1, 1), "K4", "K5", "K6", "K7", ("w", 3, 1, 1, 0),
-        "H4", "H5", "H6", "H7", ("n", 3, 0, 5, 1), ("w", 3, 1, 5, 0), ("w", 3, 1, 4, 0), ("n", 0, "x", 3, "x"),
-        ("n", 5, 0, 1, 1), "G4", "G5", "G6", "G7", ("n", 0, "z", 2, "z"), ("n", 3, 0, 2, 1),
-        ("n", 3, "x", 2, "x"), ("n", 5, 0, 2, 1),
+        "S1", "S2", "S3", "E0", "F0", "W1", "W2", "W3", "S4", "S5", "E1", "T0", "E2", "E3", "R0",
+        ("s", 0, 0, 0, 0), "W4", "W5", "S6", "S7", "F1", "F2", "F3", "E4", "E5", "E6", "E7", ("s", 0, 1, 0, 1),
+        ("n", 0, 0, 0, 1), "C3", "C4", "D0", "D1", "D2", "D3", "D4", "D5", "D6", "D7", "K0", "K1", "K2", "K3",
+        "R3", ("w", 3, 0, 4, 0), ("w", 0, 0, 4, 0), "F4", "F5", ("n", 3, 0, 0, 1), "F6", "F7", "C1",
+        ("w", 0, 0, 1, 0), ("w", 0, 1, 1, 0), ("w", 3, 0, 1, 0), "K4", "K5", "K6", "K7", ("w", 3, 1, 1, 0),
+        "C5", "H0", "H1", "H2", "H3", "H4", "H5", "H6", "H7", ("w", 3, 0, 5, 0), ("w", 3, 1, 5, 0),
+        ("w", 3, 1, 4, 0), "C2", "G0", "G1", "G2", "G3", "G4", "G5", "G6", "G7", "R2", ("w", 0, "z", 2, 0),
+        ("w", 0, 0, 5, 0), "P0", ("w", 2, 0, 5, 0), "P2", "R1", ("w", 1, 0, 5, 0), "P1", ("n", 3, "x", 0, "x"),
+        ("n", 3, 0, 2, 1), ("n", 3, "x", 2, "x"), ("p", 0, 0, 0, 0),
     ),
     (
-        "S1", "S2", "S3", "E0", "T0", "F0", "W1", "W2", "W3", "S4", "S5", "E1", "E2", "E3", "R0",
-        ("s", 0, 0, 0, 0), "G0", "W4", "W5", "S6", "S7", "F1", "F2", "F3", "C1", ("n", 0, 0, 1, 0), "E4", "E5",
-        "E6", "E7", ("s", 0, 1, 0, 1), ("n", 0, 0, 0, 1), "G1", "G2", "G3", ("n", 0, 1, 1, 0), "C2",
-        ("n", 0, 1, 2, 0), "F4", "F5", "C5", "H0", "H1", "H2", "H3", ("n", 0, 1, 5, 0), "C4", "D0", "D1", "D2",
-        "D3", ("n", 0, 1, 4, 0), "D4", "D5", "D6", "D7", ("n", 0, 1, 4, 1), "F6", "F7", ("n", 0, 0, 1, 1),
-        ("n", 0, 1, 1, 1), "R5", ("n", 5, 0, 1, 1), "H4", "H5", "H6", "H7", ("n", 0, 1, 5, 1),
-        ("n", 5, 1, 1, 1), "G4", "G5", "C3", "K0", "K1", "K2", "K3", "R3", ("n", 3, 0, 1, 0),
-        ("n", 3, 0, 1, 1), ("n", 3, 0, 5, 0), ("n", 3, 0, 5, 1), "G6", "G7", ("n", 3, 0, 4, 0),
-        ("n", 3, 0, 4, 1), ("n", 0, "z", 2, "z"), ("n", 0, 1, 3, 0), ("n", 3, 0, 2, 1), ("n", 5, 0, 2, 1),
-        ("n", 5, 1, 2, 1), "K4", "K5", "K6", "K7", ("w", 3, 1, 1, 0), ("w", 3, 1, 5, 0), ("w", 3, 1, 4, 0),
-        ("n", 0, "x", 3, "x"), ("n", 3, "x", 2, "x"),
+        "S1", "S2", "S3", "E0", "F0", "W1", "W2", "W3", "S4", "S5", "E1", "T0", "E2", "E3", "R0",
+        ("s", 0, 0, 0, 0), "G0", "W4", "W5", "S6", "S7", "F1", "F2", "F3", "E4", "E5", "E6", "E7",
+        ("s", 0, 1, 0, 1), ("n", 0, 0, 0, 1), "G1", "C4", "D4", "D5", "D6", "D7", "R4", ("w", 4, 1, 0, 0),
+        "P4", "G2", "G3", "F4", "F5", "F6", "F7", "C1", ("w", 0, 0, 1, 0), ("w", 0, 1, 1, 0), "C5", "H4", "H5",
+        "H6", "H7", "R5", ("w", 5, 1, 0, 0), "G4", "G5", ("w", 5, 1, 1, 0), "C3", "K0", "K1", "K2", "K3", "R3",
+        ("w", 3, 0, 1, 0), "H0", "H1", "H2", "H3", ("w", 3, 0, 5, 0), "G6", "G7", "D0", "D1", "D2", "D3",
+        ("w", 3, 0, 4, 0), "C2", "R2", ("w", 0, "z", 2, 0), "P0", "P2", ("w", 5, 1, 2, 0), "P5",
+        ("n", 3, 0, 0, 1), ("n", 3, 0, 2, 1), "K4", "K5", "K6", "K7", ("w", 3, 1, 1, 0), ("w", 3, 1, 5, 0),
+        ("w", 3, 1, 4, 0), ("n", 3, "x", 0, "x"), ("n", 3, "x", 2, "x"), ("p", 0, 0, 0, 0),
     ),
 )
-
-
-ROWSLOT = {0: 0, 3: 1, 5: 2}
 
 
 def kernel(
     cap, cid_ref, cg_ref, emb_ref, out_ref,
     emb, unit, hot, outgo, sh, tagout, tagin, ct, rowtag,
-    rowmax, rowsum, colmax, colsum, part, back, ids,
+    rowmax, rowsum, colmax, colsum, rowflat, part, back, ids,
     in_sem, a_s, a_r, f_s, f_r, t_s, t_r, ct_s, ct_r, b_s, b_r,
 ):
     rows, width = emb.shape
@@ -116,14 +109,16 @@
         events.append(when)
         tiles.append(work)
     count = len(tiles[0])
-    bits = {"z": z // 2, "x": xb}
+    zbit = z // 2
 
     def number(item):
         kind, i, a, j, b = item
         base = 256 * KINDS[kind] + 16 * (2 * j) + 2 * i
-        if a in bits:
-            return base, a
-        return base + a + 16 * b, None
+        if a == "z":
+            return base, zbit, 2 * j + 1 - 2 * i + 16 * (2 * i - 2 * j)
+        if a == "x":
+            return base, xb, 17
+        return base + a + 16 * b, 0, 0
 
     words = []
     for k in range(0, count, 3):
@@ -131,10 +126,8 @@
         for work in tiles:
             word = 0
             for r, item in enumerate(work[k : k + 3]):
-                base, bit = number(item)
-                word = word + base * 1024**r
-                if bit is not None:
-                    word = word + bits[bit] * (17 * 1024**r)
+                base, bit, more = number(item)
+                word = word + base * 1024**r + bit * (more * 1024**r)
             both.append(word)
         words.append(jnp.where(c == 0, both[0], both[1]))
 
@@ -145,7 +138,7 @@
             word = jnp.where(u == k, words[k], word)
         code = jnp.where(r == 0, word, jnp.where(r == 1, word // 1024, word // 1024**2)) % 1024
         kind, j, i = code // 256, code // 16 % 16, code % 16
-        return kind, i - jnp.where(i < 2, 0, jnp.where(i < 8, 4, 6)), i, j
+        return kind, i, j
 
     cid = cid_ref[...]
     group = jnp.zeros(cid.shape, jnp.int32)
@@ -188,6 +181,8 @@
     colmax[...] = jnp.full(colmax.shape, -1.0, F32)
     rowsum[...] = jnp.zeros(rowsum.shape, F32)
     colsum[...] = jnp.zeros(colsum.shape, F32)
+    rowflat[:, 0:1, :] = jnp.full((2 * SLOTS, 1, half), -1.0, F32)
+    rowflat[:, 1:2, :] = jnp.zeros((2 * SLOTS, 1, half), F32)
     part[...] = jnp.zeros(part.shape, F32)
 
     for k in range(parts):
@@ -245,7 +240,7 @@
             for k in range(half // lanes):
                 v = ct[2 * slot + a, 0:1, k * lanes : (k + 1) * lanes]
                 v = jnp.where(v == 0.0, -1.0, v)
-                rowtag[2 * ROWSLOT[slot] + a, pl.ds(k * lanes, lanes), :] = jnp.transpose(
+                rowtag[2 * slot + a, pl.ds(k * lanes, lanes), :] = jnp.transpose(
                     jnp.broadcast_to(v, (lanes, lanes))
                 )
 
@@ -256,6 +251,15 @@
         )
 
     ahead, across, sibling = dev(x, y, zf, c), dev(xn, y, z, c), dev(x, y, z, 1 - c)
+
+    def flatten(slot):
+        for n in (2 * slot, 2 * slot + 1):
+            for k in range(half // lanes):
+                at = slice(k * lanes, (k + 1) * lanes)
+                for row, ref, op in ((0, rowmax, jnp.max), (1, rowsum, jnp.sum)):
+                    rowflat[n, row : row + 1, at] = op(
+                        jnp.transpose(ref[n, at, :]), axis=0, keepdims=True
+                    )
 
     def event(kind, q):
         if kind == "T":
@@ -264,6 +268,8 @@
             return row_tags(q)
         if kind == "C":
             return landed(ct.at[pl.ds(2 * q, 2)], ct_r.at[q - 1])
+        if kind == "P":
+            return flatten(q)
         if kind == "S":
             return send_rows(q).start()
         if kind == "W":
@@ -282,9 +288,6 @@
         if slot == 2:
             pl.when(c == 1)(forward(2, 3, q, across).start)
 
-    def cut(ref, k):
-        return ref[:, k * lanes : (k + 1) * lanes]
-
     blocks = half // lanes
 
     def scores(i, j):
@@ -292,7 +295,7 @@
             sh[i], j, (((1,), (1,)), ((), ())), preferred_element_type=F32
         )
 
-    def tile(ri, i, j, halves):
+    def tile(i, j, halves):
         s = scores(i, sh[pl.ds(j, halves)].reshape(halves * half, width))
         cols = [(j + a, slice(k * lanes, (k + 1) * lanes)) for a in range(halves) for k in range(blocks)]
         cm = [colmax[n, :, at] for n, at in cols]
@@ -300,14 +303,14 @@
         tag = [ct[n, 0:1, at] for n, at in cols]
         for r in range(blocks):
             at = slice(r * lanes, (r + 1) * lanes)
-            rt, rm, rs = rowtag[ri, at, :], rowmax[ri, at, :], rowsum[ri, at, :]
+            rt, rm, rs = rowtag[i, at, :], rowmax[i, at, :], rowsum[i, at, :]
             for k in range(len(cols)):
                 v = jnp.where(rt == tag[k], s[at, k * lanes : (k + 1) * lanes], MASKED)
                 e = jnp.exp(20.0 * v)
                 rm, rs = jnp.maximum(rm, v), rs + e
                 cm[k] = jnp.maximum(cm[k], jnp.max(v.reshape(lanes // 8, 8, lanes), axis=0))
                 cs[k] = cs[k] + jnp.sum(e.reshape(lanes // 8, 8, lanes), axis=0)
-            rowmax[ri, at, :], rowsum[ri, at, :] = rm, rs
+            rowmax[i, at, :], rowsum[i, at, :] = rm, rs
         for k, (n, at) in enumerate(cols):
             colmax[n, :, at], colsum[n, :, at] = cm[k], cs[k]
 
@@ -345,28 +348,23 @@
                                 for kind, q in what:
                                     event(kind, q)
 
-        kind, ri, i, j = operands(t)
+        kind, i, j = operands(t)
 
         @pl.when(kind == 0)
         def _():
-            tile(ri, i, j, 1)
+            tile(i, j, 1)
 
         @pl.when(kind == 1)
         def _():
-            tile(ri, i, j, 2)
+            tile(i, j, 2)
 
         @pl.when(kind == 2)
         def _():
-            own_tile(ri)
+            own_tile(i)
 
         return carry
 
     lax.fori_loop(0, count, turn, 0)
-
-    def flat(ref, ri, k, op):
-        return op(
-            jnp.transpose(ref[ri, k * lanes : (k + 1) * lanes, :]), axis=0, keepdims=True
-        )
 
     places = {
         0: (x, z, c), 1: (x, zb, c), 2: (x, z2, c), 3: (xn, z3, c), 4: (x, z, 1 - c), 5: (x, zf, 1 - c),
@@ -380,18 +378,13 @@
             device_id=dev(3 - xo if sx else xo, (y - sy + 4) % 4, zo, co), device_id_type=MESH,
         )
 
-    for j in (4, 1, 2, 5, 3, 0):
+    flatten(3)
+    for j in (3, 2, 5, 1, 0, 4):
         for a in (0, 1):
             top = jnp.max(colmax[2 * j + a], axis=0, keepdims=True)
             total = jnp.sum(colsum[2 * j + a], axis=0, keepdims=True)
-            if j in ROWSLOT:
-                ri = 2 * ROWSLOT[j] + a
-                top = jnp.maximum(
-                    top, jnp.concatenate([flat(rowmax, ri, k, jnp.max) for k in range(blocks)], axis=1)
-                )
-                total = total + jnp.concatenate(
-                    [flat(rowsum, ri, k, jnp.sum) for k in range(blocks)], axis=1
-                )
+            top = jnp.maximum(top, rowflat[2 * j + a, 0:1, :])
+            total = total + rowflat[2 * j + a, 1:2, :]
             for k in range(4):
                 q = 4 * a + k
                 at = SLOTS * q + j
@@ -459,13 +452,14 @@
             pltpu.VMEM((GROUPS, 8, lanes), F32),
             pltpu.VMEM((GROUPS, 8, lanes), F32),
             pltpu.VMEM((2 * SLOTS, 8, half), F32),
-            pltpu.VMEM((6, half, lanes), F32),
-            pltpu.VMEM((6, half, lanes), F32),
-            pltpu.VMEM((6, half, lanes), F32),
+            pltpu.VMEM((2 * SLOTS, half, lanes), F32),
+            pltpu.VMEM((2 * SLOTS, half, lanes), F32),
+            pltpu.VMEM((2 * SLOTS, half, lanes), F32),
             pltpu.VMEM((2 * SLOTS, 8, half), F32),
             pltpu.VMEM((2 * SLOTS, 8, half), F32),
-            pltpu.VMEM((SLOTS * GROUPS, 8, lanes), F32),
-            pltpu.VMEM((SLOTS * GROUPS, 8, lanes), F32),
+            pltpu.VMEM((2 * SLOTS, 2, half), F32),
+            pltpu.VMEM((SLOTS * GROUPS, 2, lanes), F32),
+            pltpu.VMEM((SLOTS * GROUPS, 2, lanes), F32),
             pltpu.VMEM((2, 8, lanes), jnp.int32),
             dma((4,)),
             dma((GROUPS,)), dma((GROUPS,)),

time: 72.2 us -> 70 us (0.970)
  Pallas kernels: 71.4 us -> 69.1 us
    pallas_call x1, Pallas kernels: 70.1 us -> 67.9 us  [body(): pl.pallas_call(functools.partial(kernel, cap), out_shape=jax.ShapeDtypeSt...]
where the time goes in v4:
time: 70 us; the launch traced here: 69.8 us
  Pallas kernels  69.1 us (99%)
    pallas_call x1, Pallas kernels, body(): pl.pallas_call(functools.partial(kernel, cap), out_shape=jax.ShapeDtypeSt...  67.9 us

profile of v4, /device:TPU:1, one launch (start us, length us, event | category | flops | bytes accessed | tf_op | source)
XLA Modules:
  0.0 69.8 jit_solution(1325389297732914202)
XLA Ops:
  0.6 67.9 %shard_map.50.both_ref = f32[8,128]{1,0:T(8,128)} custom-call(s32[1,512]{1,0:T(1,128)} %bitcast.3, s32[64]{0:T(128)} %cg_ref.1, f32[512,1024]{1,0:T(8,128)} %emb_ref.1), custom_call_target="tpu_custom_call" | custom-call | tf_op jit(solution)/shard_map/pallas_call | solution.py:437
  68.5 1.3 %shard_map.51 = (f32[4,128]{1,0:T(4,128)}, f32[4,128]{1,0:T(4,128)}) custom-call(f32[8,128]{1,0:T(8,128)} %shard_map.50.both_ref), custom_call_target="tpu_custom_call" | custom-call | tf_op jit(solution)/shard_map/pallas_call | solution.py:476

commit v5 on v4

--- a/solution.py
+++ b/solution.py
@@ -19,8 +19,8 @@
 SLOT_OF = {"E": 0, "F": 1, "G": 2, "K": 3, "D": 4, "H": 5}
 PROGRAMS = (
     (
-        "S1", "S2", "S3", "E0", "F0", "W1", "W2", "W3", "S4", "S5", "E1", "T0", "E2", "E3", "R0",
-        ("s", 0, 0, 0, 0), "W4", "W5", "S6", "S7", "F1", "F2", "F3", "E4", "E5", "E6", "E7", ("s", 0, 1, 0, 1),
+        "S1", "S2", "S3", "E0", "F0", "W1", "W2", "W3", "S4", "S5", "E1", "T0", "E2", "E3",
+        "W4", "W5", "S6", "S7", "F1", "R0", ("s", 0, 0, 0, 0), "F2", "F3", "E4", "E5", "E6", "E7", ("s", 0, 1, 0, 1),
         ("n", 0, 0, 0, 1), "C3", "C4", "D0", "D1", "D2", "D3", "D4", "D5", "D6", "D7", "K0", "K1", "K2", "K3",
         "R3", ("w", 3, 0, 4, 0), ("w", 0, 0, 4, 0), "F4", "F5", ("n", 3, 0, 0, 1), "F6", "F7", "C1",
         ("w", 0, 0, 1, 0), ("w", 0, 1, 1, 0), ("w", 3, 0, 1, 0), "K4", "K5", "K6", "K7", ("w", 3, 1, 1, 0),
@@ -30,8 +30,8 @@
         ("n", 3, 0, 2, 1), ("n", 3, "x", 2, "x"), ("p", 0, 0, 0, 0),
     ),
     (
-        "S1", "S2", "S3", "E0", "F0", "W1", "W2", "W3", "S4", "S5", "E1", "T0", "E2", "E3", "R0",
-        ("s", 0, 0, 0, 0), "G0", "W4", "W5", "S6", "S7", "F1", "F2", "F3", "E4", "E5", "E6", "E7",
+        "S1", "S2", "S3", "E0", "F0", "W1", "W2", "W3", "S4", "S5", "E1", "T0", "E2", "E3",
+        "G0", "W4", "W5", "S6", "S7", "F1", "R0", ("s", 0, 0, 0, 0), "F2", "F3", "E4", "E5", "E6", "E7",
         ("s", 0, 1, 0, 1), ("n", 0, 0, 0, 1), "G1", "C4", "D4", "D5", "D6", "D7", "R4", ("w", 4, 1, 0, 0),
         "P4", "G2", "G3", "F4", "F5", "F6", "F7", "C1", ("w", 0, 0, 1, 0), ("w", 0, 1, 1, 0), "C5", "H4", "H5",
         "H6", "H7", "R5", ("w", 5, 1, 0, 0), "G4", "G5", ("w", 5, 1, 1, 0), "C3", "K0", "K1", "K2", "K3", "R3",
@@ -393,6 +393,20 @@
                 if at:
                     send_part(j, q).start()
     rest = pl.ds(1, SLOTS * GROUPS - 1)
+    for n in range(1, GROUPS):
+        send_tag(n).wait_send()
+        for core in (0, 1):
+            if ("W", n) not in sum(events[core].values(), []):
+                pl.when(c == core)(send_rows(n).wait_send)
+    for j in range(1, SLOTS):
+        send_ct(j).wait_send()
+    for q in range(GROUPS):
+        forward(0, 1, q, ahead).wait_send()
+        forward(0, 4, q, sibling).wait_send()
+        forward(1, 2, q, ahead).wait_send()
+        forward(1, 5, q, sibling).wait_send()
+        forward(0, 3, q, across).wait_send()
+    landed(part.at[rest], b_s)
     landed(back.at[rest], b_r)
 
     target8, rank8 = ids[0], ids[1]
@@ -406,21 +420,6 @@
             outs[k] = jnp.where(target8 == n, found, outs[k])
     for k in (0, 1):
         out_ref[k * rows // lanes : (k + 1) * rows // lanes] = outs[k][0 : rows // lanes]
-
-    for n in range(1, GROUPS):
-        send_tag(n).wait_send()
-        for core in (0, 1):
-            if ("W", n) not in sum(events[core].values(), []):
-                pl.when(c == core)(send_rows(n).wait_send)
-    for j in range(1, SLOTS):
-        send_ct(j).wait_send()
-    landed(part.at[rest], b_s)
-    for q in range(GROUPS):
-        forward(0, 1, q, ahead).wait_send()
-        forward(0, 4, q, sibling).wait_send()
-        forward(1, 2, q, ahead).wait_send()
-        forward(1, 5, q, sibling).wait_send()
-        forward(0, 3, q, across).wait_send()
 
 
 def part_in_two(both_ref, best_ref, mass_ref):

time: 70 us -> 69.9 us (level)
  no operation moved by 1% of the time
where the time goes in v5:
time: 69.9 us; the launch traced here: 69.7 us
  Pallas kernels  69.1 us (99%)
    pallas_call x1, Pallas kernels, body(): pl.pallas_call(functools.partial(kernel, cap), out_shape=jax.ShapeDtypeSt...  67.8 us

profile of v5, /device:TPU:1, one launch (start us, length us, event | category | flops | bytes accessed | tf_op | source)
XLA Modules:
  0.0 69.7 jit_solution(8998290164687166103)
XLA Ops:
  0.6 67.8 %shard_map.50.both_ref = f32[8,128]{1,0:T(8,128)} custom-call(s32[1,512]{1,0:T(1,128)} %bitcast.3, s32[64]{0:T(128)} %cg_ref.1, f32[512,1024]{1,0:T(8,128)} %emb_ref.1), custom_call_target="tpu_custom_call" | custom-call | tf_op jit(solution)/shard_map/pallas_call | solution.py:436
  68.4 1.3 %shard_map.51 = (f32[4,128]{1,0:T(4,128)}, f32[4,128]{1,0:T(4,128)}) custom-call(f32[8,128]{1,0:T(8,128)} %shard_map.50.both_ref), custom_call_target="tpu_custom_call" | custom-call | tf_op jit(solution)/shard_map/pallas_call | solution.py:475

commit v6 on v4

--- a/solution.py
+++ b/solution.py
@@ -35,7 +35,7 @@
         ("s", 0, 1, 0, 1), ("n", 0, 0, 0, 1), "G1", "C4", "D4", "D5", "D6", "D7", "R4", ("w", 4, 1, 0, 0),
         "P4", "G2", "G3", "F4", "F5", "F6", "F7", "C1", ("w", 0, 0, 1, 0), ("w", 0, 1, 1, 0), "C5", "H4", "H5",
         "H6", "H7", "R5", ("w", 5, 1, 0, 0), "G4", "G5", ("w", 5, 1, 1, 0), "C3", "K0", "K1", "K2", "K3", "R3",
-        ("w", 3, 0, 1, 0), "H0", "H1", "H2", "H3", ("w", 3, 0, 5, 0), "G6", "G7", "D0", "D1", "D2", "D3",
+        ("w", 3, 0, 1, 0), "H0", "H1", "H2", "H3", "G6", ("w", 3, 0, 5, 0), "G7", "D0", "D1", "D2", "D3",
         ("w", 3, 0, 4, 0), "C2", "R2", ("w", 0, "z", 2, 0), "P0", "P2", ("w", 5, 1, 2, 0), "P5",
         ("n", 3, 0, 0, 1), ("n", 3, 0, 2, 1), "K4", "K5", "K6", "K7", ("w", 3, 1, 1, 0), ("w", 3, 1, 5, 0),
         ("w", 3, 1, 4, 0), ("n", 3, "x", 0, "x"), ("n", 3, "x", 2, "x"), ("p", 0, 0, 0, 0),

time: 70 us -> 70 us (level)
  no operation moved by 1% of the time
where the time goes in v6:
time: 70 us; the launch traced here: 69.8 us
  Pallas kernels  69.1 us (99%)
    pallas_call x1, Pallas kernels, body(): pl.pallas_call(functools.partial(kernel, cap), out_shape=jax.ShapeDtypeSt...  67.9 us

profile of v6, /device:TPU:1, one launch (start us, length us, event | category | flops | bytes accessed | tf_op | source)
XLA Modules:
  0.0 69.8 jit_solution(12778631995789022086)
XLA Ops:
  0.6 67.9 %shard_map.50.both_ref = f32[8,128]{1,0:T(8,128)} custom-call(s32[1,512]{1,0:T(1,128)} %bitcast.3, s32[64]{0:T(128)} %cg_ref.1, f32[512,1024]{1,0:T(8,128)} %emb_ref.1), custom_call_target="tpu_custom_call" | custom-call | tf_op jit(solution)/shard_map/pallas_call | solution.py:437
  68.5 1.3 %shard_map.51 = (f32[4,128]{1,0:T(4,128)}, f32[4,128]{1,0:T(4,128)}) custom-call(f32[8,128]{1,0:T(8,128)} %shard_map.50.both_ref), custom_call_target="tpu_custom_call" | custom-call | tf_op jit(solution)/shard_map/pallas_call | solution.py:476
